TPU v7x, 256 devices: a whole 4x4x8 slice. The times are simulated.
256 devices in a mesh: ctx: 32 (over z, y_lo, core), head: 8 (over x, y_hi).
Axes of the slice: x: 4, y: 4 (y_hi: 2, y_lo: 2; y = y_hi * 2 + y_lo), z: 8, core: 2. Of those that a mesh axis runs over, the one named last changes fastest.
Arguments:
- query_nope: bfloat16 [8192, 16384], P('ctx', 'head'), may hold values from -6 to 6
- query_rope: bfloat16 [8192, 8192], P('ctx', 'head'), may hold values from -300 to 300, as said below
- latent: bfloat16 [8192, 576], P(('ctx', 'head')), may hold values from -6 to 6, as said below
- key_up: bfloat16 [512, 16384], P(None, 'head'), may hold values from -0.25 to 0.25
- value_up: bfloat16 [512, 16384], P(None, 'head'), may hold values from -0.25 to 0.25
- doc_lengths: int32 [8], replicated, may hold values from 1 to 3072, 8192 in all
- owner: int32 [8192], P('ctx'), may hold values from 0 to 8191, as said below
Outputs:
- attended: bfloat16 [8192, 16384], P('ctx', 'head')
Inputs may be any that keep to these rules, and one draw needn't show every extreme that they name: `doc_lengths`: positive lengths that sum to 8192; the longest is exactly 3072. `owner`: a permutation of the rows; the 256 tokens of each block of the sequence go in equal numbers to every block's rows. `latent`: finite values. `query_rope`: finite values.
All inputs are finite; a program needn't handle non-finite values.
Results may differ from a plain program's by a relative error of at most 0.0058.
Values may be sent and summed in bfloat16 or wider, within the bound.
A program may use at most 128 MiB of HBM per device.

v0:
```python
import jax
import jax.numpy as jnp
from jax import lax
from jax.sharding import PartitionSpec as P

LATENT = 512
ROPE = 64
NOPE = 128
VDIM = 128
SHIFTS = 4


def from_behind(x, axis, by):
    peers = lax.axis_size(axis)
    pairs = [(i, i + by) for i in range(peers) if 0 <= i + by < peers]
    return lax.ppermute(x, axis, pairs)


def segment_of(positions, doc_lengths):
    ends = jnp.cumsum(doc_lengths)
    return jnp.sum((ends[None, :] <= positions[:, None]).astype(jnp.int32), axis=1)


def carry_back(block):
    pieces = [block]
    current = block
    for step in range(SHIFTS):
        current = from_behind(current, "ctx", 1)
        pieces.append(current)
    return pieces


def per_device(query_nope, query_rope, latent, key_up, value_up, doc_lengths, owner):
    rows = query_nope.shape[0]
    heads_here = query_nope.shape[1] // NOPE
    window = SHIFTS * rows
    span = (SHIFTS + 1) * rows
    here = lax.axis_index("ctx")
    scale = 1.0 / float(NOPE + ROPE) ** 0.5
    whole = lax.all_gather(latent, "head", axis=0, tiled=True)
    pieces = carry_back(whole)
    context = jnp.concatenate(pieces[::-1], axis=0)
    query_pos = here * rows + jnp.arange(rows, dtype=jnp.int32)
    key_pos = (here - SHIFTS) * rows + jnp.arange(span, dtype=jnp.int32)
    query_seg = segment_of(query_pos, doc_lengths)
    key_seg = segment_of(jnp.maximum(key_pos, 0), doc_lengths)
    offset = query_pos[:, None] - key_pos[None, :]
    visible = (
        (key_pos[None, :] >= 0)
        & (offset >= 0)
        & (offset < window)
        & (query_seg[:, None] == key_seg[None, :])
    )
    compressed = context[:, :LATENT]
    keys_part = jnp.dot(compressed, key_up, preferred_element_type=jnp.float32).astype(jnp.bfloat16)
    values_part = jnp.dot(compressed, value_up, preferred_element_type=jnp.float32).astype(
        jnp.bfloat16
    )
    key_rope = context[:, LATENT:]
    group = min(4, heads_here)
    groups = heads_here // group

    def group_out(index, output):
        q_part = lax.dynamic_slice_in_dim(
            query_nope, index * group * NOPE, group * NOPE, 1
        ).reshape(rows, group, NOPE)
        r_part = lax.dynamic_slice_in_dim(
            query_rope, index * group * ROPE, group * ROPE, 1
        ).reshape(rows, group, ROPE)
        k_part = lax.dynamic_slice_in_dim(keys_part, index * group * NOPE, group * NOPE, 1).reshape(
            span, group, NOPE
        )
        v_part = lax.dynamic_slice_in_dim(
            values_part, index * group * VDIM, group * VDIM, 1
        ).reshape(span, group, VDIM)
        scores = jnp.einsum("ihd,jhd->hij", q_part, k_part, preferred_element_type=jnp.float32)
        scores = scores + jnp.einsum(
            "ihd,jd->hij", r_part, key_rope, preferred_element_type=jnp.float32
        )
        masked = jnp.where(visible[None], scores * scale, -1e30)
        largest = jnp.max(masked, axis=2, keepdims=True)
        probs = jnp.where(visible[None], jnp.exp(masked - largest), 0.0)
        total = jnp.sum(probs, axis=2)
        summed = jnp.einsum(
            "hij,jhd->ihd", probs.astype(jnp.bfloat16), v_part, preferred_element_type=jnp.float32
        )
        result = (
            (summed / jnp.transpose(total)[:, :, None])
            .astype(jnp.bfloat16)
            .reshape(rows, group * VDIM)
        )
        return lax.dynamic_update_slice_in_dim(output, result, index * group * VDIM, 1)

    attended = lax.fori_loop(
        0, groups, group_out, jnp.zeros((rows, heads_here * VDIM), jnp.bfloat16)
    )
    owners_all = lax.all_gather(owner, "ctx", axis=0, tiled=True)
    sending = jnp.argsort(owner)
    outgoing = jnp.take(attended, sending, axis=0)
    arrived = lax.all_to_all(outgoing, "ctx", split_axis=0, concat_axis=0, tiled=True)
    every = owners_all.shape[0]
    source_of = (
        jnp.zeros((every,), jnp.int32).at[owners_all].set(jnp.arange(every, dtype=jnp.int32))
    )
    local_slots = jnp.arange(rows, dtype=jnp.int32)
    sources = jnp.take(source_of, here * rows + local_slots)
    arrival_key = sources // rows * rows + local_slots
    placing = jnp.argsort(arrival_key)
    return jnp.zeros((rows, heads_here * VDIM), jnp.bfloat16).at[placing].set(arrived)


def solution(mesh):
    in_specs = (
        P("ctx", "head"),
        P("ctx", "head"),
        P(("ctx", "head"), None),
        P(None, "head"),
        P(None, "head"),
        P(),
        P("ctx"),
    )
    out_specs = P("ctx", "head")
    return jax.shard_map(
        per_device, mesh=mesh, in_specs=in_specs, out_specs=out_specs, check_vma=False
    )
```

profile of v0, /device:TPU:1, one launch (start us, length us, event | category | flops | bytes accessed | tf_op | source)
XLA Modules:
  0.0 297.7 jit_solution(16260451505614030584)
XLA Ops:
  0.0 29.9 %all_gather.7 = bf16[256,576]{1,0:T(8,128)(2,1)S(1)} all-gather(bf16[32,576]{1,0:T(8,128)(2,1)} %param.11), channel_id=1, replica_groups=mesh['ctx'=32,'head'=8] {'head'}, dimensions={0}, use_global_device_ids=true | all-gather | bytes 331776 | tf_op jit(solution)/shard_map/all_gather | solution.py:40
  29.9 9.6 %collective-permute-start = (bf16[256,576]{1,0:T(8,128)(2,1)S(1)}, bf16[256,576]{1,0:T(8,128)(2,1)S(1)}, u32[]{:S(2)}, u32[]{:S(2)}) collective-permute-start(bf16[256,576]{1,0:T(8,128)(2,1)S(1)} %all_gather.7), channel_id=1, source_target_pairs={{0,8},{8,16},{16,24},{24,32},{32,40},{40,48},{48,56},{56,64},{64,7... | collective-permute-start | bytes 884744 | tf_op jit(solution)/shard_map/ppermute | solution.py:16
  40.4 3.8 %sort.32 = (s32[256]{0:T(256)}, s32[256]{0:T(256)S(1)}) sort(s32[256]{0:T(256)} %param.15, s32[256]{0:T(256)S(1)} %iota.35), dimensions={0}, to_apply=%region_2.3 | sort | flops 2048 | bytes 4096 | tf_op jit(solution)/shard_map/jit(argsort)/sort | solution.py:98
  45.5 2.4 collective-permute-start.1
  47.9 4.0 %collective-permute-done.1 = bf16[256,576]{1,0:T(8,128)(2,1)S(1)} collective-permute-done((bf16[256,576]{1,0:T(8,128)(2,1)S(1)}, bf16[256,576]{1,0:T(8,128)(2,1)S(1)}, u32[]{:S(2)}, u32[]{:S(2)}) %collective-permute-start.1) | collective-permute-done | bytes 294944 | tf_op jit(solution)/shard_map/ppermute | solution.py:16
  51.9 4.4 %collective-permute-start.2 = (bf16[256,576]{1,0:T(8,128)(2,1)S(1)}, bf16[256,576]{1,0:T(8,128)(2,1)S(1)}, u32[]{:S(2)}, u32[]{:S(2)}) collective-permute-start(bf16[256,576]{1,0:T(8,128)(2,1)S(1)} %collective-permute-done.1), channel_id=1, source_target_pairs={{0,8},{8,16},{16,24},{24,32},{32,40},{40,48},{48,56},{56,64},{64,7... | collective-permute-start | bytes 884744 | tf_op jit(solution)/shard_map/ppermute | solution.py:16
  56.9 3.4 %collective-permute-done.2 = bf16[256,576]{1,0:T(8,128)(2,1)S(1)} collective-permute-done((bf16[256,576]{1,0:T(8,128)(2,1)S(1)}, bf16[256,576]{1,0:T(8,128)(2,1)S(1)}, u32[]{:S(2)}, u32[]{:S(2)}) %collective-permute-start.2) | collective-permute-done | bytes 294944 | tf_op jit(solution)/shard_map/ppermute | solution.py:16
  60.3 4.4 %collective-permute-start.3 = (bf16[256,576]{1,0:T(8,128)(2,1)S(1)}, bf16[256,576]{1,0:T(8,128)(2,1)S(1)}, u32[]{:S(2)}, u32[]{:S(2)}) collective-permute-start(bf16[256,576]{1,0:T(8,128)(2,1)S(1)} %collective-permute-done.2), channel_id=1, source_target_pairs={{0,8},{8,16},{16,24},{24,32},{32,40},{40,48},{48,56},{56,64},{64,7... | collective-permute-start | bytes 884744 | tf_op jit(solution)/shard_map/ppermute | solution.py:16
  65.4 3.2 %collective-permute-done.3 = bf16[256,576]{1,0:T(8,128)(2,1)S(1)} collective-permute-done((bf16[256,576]{1,0:T(8,128)(2,1)S(1)}, bf16[256,576]{1,0:T(8,128)(2,1)S(1)}, u32[]{:S(2)}, u32[]{:S(2)}) %collective-permute-start.3) | collective-permute-done | bytes 294944 | tf_op jit(solution)/shard_map/ppermute | solution.py:16
  69.0 4.7 %convolution_convert_fusion = bf16[1280,2048]{1,0:T(8,128)(2,1)} fusion(bf16[512,2048]{1,0:T(8,128)(2,1)S(1)} %copy-done, bf16[1280,576]{1,0:T(8,128)(2,1)S(1)} %constant_dynamic-update-slice_fusion.1), kind=kOutput, calls=%fused_computation.33 | convolution fusion | flops 2686976000 | bytes 8650752 | tf_op jit(solution)/shard_map/dot_general | solution.py:55
  73.7 4.6 %convolution_convert_fusion.1 = bf16[1280,2048]{1,0:T(8,128)(2,1)} fusion(bf16[512,2048]{1,0:T(8,128)(2,1)S(1)} %copy-done.11, bf16[1280,576]{1,0:T(8,128)(2,1)S(1)} %constant_dynamic-update-slice_fusion.1), kind=kOutput, calls=%fused_computation.34 | convolution fusion | flops 2686976000 | bytes 8650752 | tf_op jit(solution)/shard_map/dot_general | solution.py:56
  80.2 104.5 %while.16 = (s32[]{:T(128)}, bf16[256,2048]{1,0:T(8,128)(2,1)}, bf16[1280,2048]{1,0:T(8,128)(2,1)}, bf16[256,2048]{1,0:T(8,128)(2,1)}, bf16[1280,2048]{1,0:T(8,1...) while((s32[]{:T(128)}, bf16[256,2048]{1,0:T(8,128)(2,1)}, ...), condition=%wide.region_9.10_spmd.clone, body=%wide.region_6.9_spmd.clone.sunk | while | flops 853216768 | bytes 72686320 | solution.py:94
  80.2 3.4 %constant_dynamic-slice_fusion.7 = (bf16[1280,512]{1,0:T(8,128)(2,1)}, bf16[1280,512]{1,0:T(8,128)(2,1)}) fusion(bf16[1280,2048]{1,0:T(8,128)(2,1)} %get-tuple-element.433, s32[]{:T(128)S(6)} %select_n.134, bf16[1280,2048]{1,0:T(8,128)(2,1)} %get-tuple-element.431), kind=kLoop, calls=%fused_computation.28.clone.1 | loop fusion | bytes 5242884 | tf_op jit(solution)/shard_map/while/body/eval_jaxpr/dynamic_slice | solution.py:70
  83.5 1.6 copy.56
  85.1 1.7 constant_dynamic-slice_fusion.9
  86.8 1.8 copy.55
  88.6 1.6 constant_dynamic-slice_fusion.8
  91.2 1.8 fusion.67
  93.1 1.2 fusion.66
  94.3 1.4 fusion.68
  95.7 1.6 fusion.69
  98.1 1.5 copy.53
  99.6 5.8 %fusion.70 = bf16[256,4,128]{0,2,1:T(8,128)(2,1)S(1)} fusion(bf16[1280,4,128]{0,2,1:T(8,128)(2,1)} %bitcast.70, pred[256,1280]{1,0:T(8,128)(4,1)} %copy-done.3, f32[4,256,1280]{2,1,0:T(8,128)} %copy-done.1, f32[256,4]{0,1:T(4,128)S(1)} %bitcast.80), kind=kOutput, calls=%fused_computation.23.clone.1 | convolution fusion | flops 339740928 | bytes 7147520 | tf_op jit(solution)/shard_map/while/body/eval_jaxpr/hij,jhd->ihd/dot_general | solution.py:84
  106.3 3.4 %constant_dynamic-slice_fusion.7 = (bf16[1280,512]{1,0:T(8,128)(2,1)}, bf16[1280,512]{1,0:T(8,128)(2,1)}) fusion(bf16[1280,2048]{1,0:T(8,128)(2,1)} %get-tuple-element.433, s32[]{:T(128)S(6)} %select_n.134, bf16[1280,2048]{1,0:T(8,128)(2,1)} %get-tuple-element.431), kind=kLoop, calls=%fused_computation.28.clone.1 | loop fusion | bytes 5242884 | tf_op jit(solution)/shard_map/while/body/eval_jaxpr/dynamic_slice | solution.py:70
  109.6 1.6 copy.56
  111.2 1.7 constant_dynamic-slice_fusion.9
  112.9 1.8 copy.55
  114.7 1.6 constant_dynamic-slice_fusion.8
  117.3 1.8 fusion.67
  119.2 1.2 fusion.66
  120.4 1.4 fusion.68
  121.9 1.6 fusion.69
  124.2 1.5 copy.53
  125.7 5.8 %fusion.70 = bf16[256,4,128]{0,2,1:T(8,128)(2,1)S(1)} fusion(bf16[1280,4,128]{0,2,1:T(8,128)(2,1)} %bitcast.70, pred[256,1280]{1,0:T(8,128)(4,1)} %copy-done.3, f32[4,256,1280]{2,1,0:T(8,128)} %copy-done.1, f32[256,4]{0,1:T(4,128)S(1)} %bitcast.80), kind=kOutput, calls=%fused_computation.23.clone.1 | convolution fusion | flops 339740928 | bytes 7147520 | tf_op jit(solution)/shard_map/while/body/eval_jaxpr/hij,jhd->ihd/dot_general | solution.py:84
  132.4 3.4 %constant_dynamic-slice_fusion.7 = (bf16[1280,512]{1,0:T(8,128)(2,1)}, bf16[1280,512]{1,0:T(8,128)(2,1)}) fusion(bf16[1280,2048]{1,0:T(8,128)(2,1)} %get-tuple-element.433, s32[]{:T(128)S(6)} %select_n.134, bf16[1280,2048]{1,0:T(8,128)(2,1)} %get-tuple-element.431), kind=kLoop, calls=%fused_computation.28.clone.1 | loop fusion | bytes 5242884 | tf_op jit(solution)/shard_map/while/body/eval_jaxpr/dynamic_slice | solution.py:70
  135.8 1.6 copy.56
  137.4 1.7 constant_dynamic-slice_fusion.9
  139.1 1.8 copy.55
  140.9 1.6 constant_dynamic-slice_fusion.8
  143.5 1.8 fusion.67
  145.3 1.2 fusion.66
  146.6 1.4 fusion.68
  148.0 1.6 fusion.69
  150.3 1.5 copy.53
  151.8 5.8 %fusion.70 = bf16[256,4,128]{0,2,1:T(8,128)(2,1)S(1)} fusion(bf16[1280,4,128]{0,2,1:T(8,128)(2,1)} %bitcast.70, pred[256,1280]{1,0:T(8,128)(4,1)} %copy-done.3, f32[4,256,1280]{2,1,0:T(8,128)} %copy-done.1, f32[256,4]{0,1:T(4,128)S(1)} %bitcast.80), kind=kOutput, calls=%fused_computation.23.clone.1 | convolution fusion | flops 339740928 | bytes 7147520 | tf_op jit(solution)/shard_map/while/body/eval_jaxpr/hij,jhd->ihd/dot_general | solution.py:84
  158.5 3.4 %constant_dynamic-slice_fusion.7 = (bf16[1280,512]{1,0:T(8,128)(2,1)}, bf16[1280,512]{1,0:T(8,128)(2,1)}) fusion(bf16[1280,2048]{1,0:T(8,128)(2,1)} %get-tuple-element.433, s32[]{:T(128)S(6)} %select_n.134, bf16[1280,2048]{1,0:T(8,128)(2,1)} %get-tuple-element.431), kind=kLoop, calls=%fused_computation.28.clone.1 | loop fusion | bytes 5242884 | tf_op jit(solution)/shard_map/while/body/eval_jaxpr/dynamic_slice | solution.py:70
  161.9 1.6 copy.56
  163.5 1.7 constant_dynamic-slice_fusion.9
  165.2 1.8 copy.55
  167.0 1.6 constant_dynamic-slice_fusion.8
  169.6 1.8 fusion.67
  171.4 1.2 fusion.66
  172.7 1.4 fusion.68
  174.1 1.6 fusion.69
  176.5 1.5 copy.53
  177.9 5.8 %fusion.70 = bf16[256,4,128]{0,2,1:T(8,128)(2,1)S(1)} fusion(bf16[1280,4,128]{0,2,1:T(8,128)(2,1)} %bitcast.70, pred[256,1280]{1,0:T(8,128)(4,1)} %copy-done.3, f32[4,256,1280]{2,1,0:T(8,128)} %copy-done.1, f32[256,4]{0,1:T(4,128)S(1)} %bitcast.80), kind=kOutput, calls=%fused_computation.23.clone.1 | convolution fusion | flops 339740928 | bytes 7147520 | tf_op jit(solution)/shard_map/while/body/eval_jaxpr/hij,jhd->ihd/dot_general | solution.py:84
  184.6 3.9 %gather_fusion.1 = bf16[256,2048]{1,0:T(8,128)(2,1)S(1)} fusion(bf16[256,2048]{1,0:T(8,128)(2,1)} %get-tuple-element.208, s32[1024]{0:T(1024)} %get-tuple-element.314), kind=kCustom, calls=%fused_computation.1 | custom fusion | bytes 2098176 | tf_op jit(solution)/shard_map/jit(_take)/gather | solution.py:99
  188.5 1.1 bitcast_select_fusion
  189.7 18.4 %all-to-all-start = ((bf16[32,8,2048]{2,1,0:T(8,128)(2,1)}), bf16[32,8,2048]{2,1,0:T(8,128)(2,1)S(1)}, u32[]{:S(2)}, u32[]{:S(2)}) async-start(bf16[32,8,2048]{2,1,0:T(8,128)(2,1)} %bitcast_select_fusion), calls=%async_computation | async-start | bytes 2097152 | tf_op jit(solution)/shard_map/all_to_all | solution.py:100
  208.0 50.9 %all-gather = s32[32,1,256]{2,1,0:T(1,128)S(1)} all-gather(s32[1,1,256]{2,1,0:T(1,128)S(1)} %bitcast.75), channel_id=1, replica_groups=mesh['ctx'=32,'head'=8] {'ctx'}, dimensions={0}, use_global_device_ids=true | all-gather | bytes 33792 | tf_op jit(solution)/shard_map/all_gather | solution.py:97
  259.0 30.5 %scatter_custom_fusion = s32[8192]{0:T(1024)S(1)} fusion(s32[8192]{0:T(1024)S(1)} %compare_select_fusion, s32[8192]{0:T(1024)S(1)} %iota.31, s32[]{:T(128)} %constant.163.clone.1), kind=kCustom, calls=%fused_computation.43 | custom fusion | bytes 32772 | tf_op jit(solution)/shard_map/scatter | solution.py:103
  289.5 1.9 gather_fusion
  291.4 3.2 %sort.31 = (s32[256]{0:T(256)}, s32[256]{0:T(256)S(1)}) sort(s32[256]{0:T(256)S(1)} %iota_add_fusion.1, s32[256]{0:T(256)S(1)} %iota.34), dimensions={0}, to_apply=%region_1.2 | sort | flops 2048 | bytes 4096 | tf_op jit(solution)/shard_map/jit(argsort)/sort | solution.py:108
  294.6 3.1 %scatter_custom_fusion.1 = bf16[256,2048]{1,0:T(8,128)(2,1)} fusion(s32[256]{0:T(256)S(1)} %compare_select_fusion.3, bf16[32,8,2048]{2,1,0:T(8,128)(2,1)S(1)} %all-to-all-done, bf16[]{:T(256)} %constant.159.clone.1), kind=kCustom, calls=%fused_computation.37 | custom fusion | bytes 2097154 | tf_op jit(solution)/shard_map/scatter | solution.py:109
  (112 shorter events, 16.3 us)
Async XLA Ops:
  0.0 68.9 %copy-start = (bf16[512,2048]{1,0:T(8,128)(2,1)S(1)}, bf16[512,2048]{1,0:T(8,128)(2,1)}, u32[]{:S(2)}) copy-start(bf16[512,2048]{1,0:T(8,128)(2,1)} %param.12) | copy-start | bytes 6291460
  29.9 15.6 %collective-permute-start = (bf16[256,576]{1,0:T(8,128)(2,1)S(1)}, bf16[256,576]{1,0:T(8,128)(2,1)S(1)}, u32[]{:S(2)}, u32[]{:S(2)}) collective-permute-start(bf16[256,576]{1,0:T(8,128)(2,1)S(1)} %all_gather.7), channel_id=1, source_target_pairs={{0,8},{8,16},{16,24},{24,32},{32,40},{40,48},{48,56},{56,64},{64,7... | collective-permute-start | bytes 884744 | tf_op jit(solution)/shard_map/ppermute | solution.py:16
  45.5 6.4 %collective-permute-start.1 = (bf16[256,576]{1,0:T(8,128)(2,1)S(1)}, bf16[256,576]{1,0:T(8,128)(2,1)S(1)}, u32[]{:S(2)}, u32[]{:S(2)}) collective-permute-start(bf16[256,576]{1,0:T(8,128)(2,1)S(1)} %collective-permute-done), channel_id=1, source_target_pairs={{0,8},{8,16},{16,24},{24,32},{32,40},{40,48},{48,56},{56,64},{64,7... | collective-permute-start | bytes 884744 | tf_op jit(solution)/shard_map/ppermute | solution.py:16
  51.9 8.4 %collective-permute-start.2 = (bf16[256,576]{1,0:T(8,128)(2,1)S(1)}, bf16[256,576]{1,0:T(8,128)(2,1)S(1)}, u32[]{:S(2)}, u32[]{:S(2)}) collective-permute-start(bf16[256,576]{1,0:T(8,128)(2,1)S(1)} %collective-permute-done.1), channel_id=1, source_target_pairs={{0,8},{8,16},{16,24},{24,32},{32,40},{40,48},{48,56},{56,64},{64,7... | collective-permute-start | bytes 884744 | tf_op jit(solution)/shard_map/ppermute | solution.py:16
  60.3 8.4 %collective-permute-start.3 = (bf16[256,576]{1,0:T(8,128)(2,1)S(1)}, bf16[256,576]{1,0:T(8,128)(2,1)S(1)}, u32[]{:S(2)}, u32[]{:S(2)}) collective-permute-start(bf16[256,576]{1,0:T(8,128)(2,1)S(1)} %collective-permute-done.2), channel_id=1, source_target_pairs={{0,8},{8,16},{16,24},{24,32},{32,40},{40,48},{48,56},{56,64},{64,7... | collective-permute-start | bytes 884744 | tf_op jit(solution)/shard_map/ppermute | solution.py:16
  68.9 4.7 %copy-start.11 = (bf16[512,2048]{1,0:T(8,128)(2,1)S(1)}, bf16[512,2048]{1,0:T(8,128)(2,1)}, u32[]{:S(2)}) copy-start(bf16[512,2048]{1,0:T(8,128)(2,1)} %param.13) | copy-start | bytes 6291460
  80.2 3.4 %copy-start.6 = (s32[256]{0:T(256)}, s32[256]{0:T(256)S(1)}, u32[]{:S(2)}) copy-start(s32[256]{0:T(256)S(1)} %get-tuple-element.438) | copy-start | bytes 3076 | tf_op jit(solution)/shard_map/while
  91.2 1.9 copy-start.5
  91.2 1.9 copy-start.8
  91.2 3.1 %copy-start.4 = (bf16[256,512]{0,1:T(8,128)(2,1)S(1)}, bf16[256,512]{0,1:T(8,128)(2,1)}, u32[]{:S(2)}) copy-start(bf16[256,512]{0,1:T(8,128)(2,1)} %copy.55) | copy-start | bytes 786436 | tf_op jit(solution)/shard_map/while
  94.3 1.4 copy-start.3
  95.7 2.4 copy-start.1
  95.7 2.4 copy-start.2
  99.6 6.7 %copy-start.7 = (s32[256]{0:T(256)S(1)}, s32[256]{0:T(256)}, u32[]{:S(2)}) copy-start(s32[256]{0:T(256)} %copy-done.6) | copy-start | bytes 3076 | tf_op jit(solution)/shard_map/while
  106.3 3.4 %copy-start.6 = (s32[256]{0:T(256)}, s32[256]{0:T(256)S(1)}, u32[]{:S(2)}) copy-start(s32[256]{0:T(256)S(1)} %get-tuple-element.438) | copy-start | bytes 3076 | tf_op jit(solution)/shard_map/while
  117.3 1.9 copy-start.5
  117.3 1.9 copy-start.8
  117.3 3.1 %copy-start.4 = (bf16[256,512]{0,1:T(8,128)(2,1)S(1)}, bf16[256,512]{0,1:T(8,128)(2,1)}, u32[]{:S(2)}) copy-start(bf16[256,512]{0,1:T(8,128)(2,1)} %copy.55) | copy-start | bytes 786436 | tf_op jit(solution)/shard_map/while
  120.4 1.4 copy-start.3
  121.8 2.4 copy-start.1
  121.9 2.4 copy-start.2
  125.7 6.7 %copy-start.7 = (s32[256]{0:T(256)S(1)}, s32[256]{0:T(256)}, u32[]{:S(2)}) copy-start(s32[256]{0:T(256)} %copy-done.6) | copy-start | bytes 3076 | tf_op jit(solution)/shard_map/while
  132.4 3.4 %copy-start.6 = (s32[256]{0:T(256)}, s32[256]{0:T(256)S(1)}, u32[]{:S(2)}) copy-start(s32[256]{0:T(256)S(1)} %get-tuple-element.438) | copy-start | bytes 3076 | tf_op jit(solution)/shard_map/while
  143.4 1.9 copy-start.5
  143.5 1.9 copy-start.8
  143.5 3.1 %copy-start.4 = (bf16[256,512]{0,1:T(8,128)(2,1)S(1)}, bf16[256,512]{0,1:T(8,128)(2,1)}, u32[]{:S(2)}) copy-start(bf16[256,512]{0,1:T(8,128)(2,1)} %copy.55) | copy-start | bytes 786436 | tf_op jit(solution)/shard_map/while
  146.6 1.4 copy-start.3
  148.0 2.4 copy-start.1
  148.0 2.4 copy-start.2
  151.8 6.7 %copy-start.7 = (s32[256]{0:T(256)S(1)}, s32[256]{0:T(256)}, u32[]{:S(2)}) copy-start(s32[256]{0:T(256)} %copy-done.6) | copy-start | bytes 3076 | tf_op jit(solution)/shard_map/while
  158.5 3.4 %copy-start.6 = (s32[256]{0:T(256)}, s32[256]{0:T(256)S(1)}, u32[]{:S(2)}) copy-start(s32[256]{0:T(256)S(1)} %get-tuple-element.438) | copy-start | bytes 3076 | tf_op jit(solution)/shard_map/while
  169.6 1.9 copy-start.5
  169.6 1.9 copy-start.8
  169.6 3.1 %copy-start.4 = (bf16[256,512]{0,1:T(8,128)(2,1)S(1)}, bf16[256,512]{0,1:T(8,128)(2,1)}, u32[]{:S(2)}) copy-start(bf16[256,512]{0,1:T(8,128)(2,1)} %copy.55) | copy-start | bytes 786436 | tf_op jit(solution)/shard_map/while
  172.7 1.4 copy-start.3
  174.1 2.4 copy-start.1
  174.1 2.4 copy-start.2
  177.9 6.7 %copy-start.7 = (s32[256]{0:T(256)S(1)}, s32[256]{0:T(256)}, u32[]{:S(2)}) copy-start(s32[256]{0:T(256)} %copy-done.6) | copy-start | bytes 3076 | tf_op jit(solution)/shard_map/while
  184.6 3.9 %copy-start.9 = (pred[32,8]{1,0:T(8,128)(4,1)S(1)}, pred[32,8]{1,0:T(8,128)(4,1)}, u32[]{:S(2)}) copy-start(pred[32,8]{1,0:T(8,128)(4,1)} %broadcast_in_dim.91) | copy-start | bytes 772
  188.5 19.5 %copy-start.10 = (s32[256]{0:T(256)S(1)}, s32[256]{0:T(256)}, u32[]{:S(2)}) copy-start(s32[256]{0:T(256)} %param.15) | copy-start | bytes 3076
  189.7 104.9 %all-to-all-start = ((bf16[32,8,2048]{2,1,0:T(8,128)(2,1)}), bf16[32,8,2048]{2,1,0:T(8,128)(2,1)S(1)}, u32[]{:S(2)}, u32[]{:S(2)}) async-start(bf16[32,8,2048]{2,1,0:T(8,128)(2,1)} %bitcast_select_fusion), calls=%async_computation | async-start | bytes 2097152 | tf_op jit(solution)/shard_map/all_to_all | solution.py:100
where the time goes:
time: 299 us; the launch traced here: 298 us
  local copies, waits for them, and re-layouts  98.7 us (33%)
  blocking collectives  80.8 us (27%)
  matrix products  45.4 us (15%)
  starting transfers between devices  39.1 us (13%)
  other arithmetic  22.3 us (7%)
  waiting for transfers between devices  10.6 us (4%)
    all_gather x1, blocking collectives, per_device(): owners_all = lax.all_gather(owner, 'ctx', axis=0, tiled=True)  50.9 us
    scatter x1, local copies, waits for them, and re-layouts, per_device(): jnp.zeros((every,), jnp.int32).at[owners_all]  30.5 us
    all_gather x1, blocking collectives, per_device(): whole = lax.all_gather(latent, 'head', axis=0, tiled=True)  29.9 us
    dot_general x4, matrix products, group_out(): jnp.einsum('hij,jhd->ihd', probs.astype(jnp.bfloat16), v_part, preferred_...  23.3 us
    ppermute x4, starting transfers between devices, from_behind(): return lax.ppermute(x, axis, pairs)  20.7 us
    dynamic_slice x8, local copies, waits for them, and re-layouts, group_out(): lax.dynamic_slice_in_dim(keys_part, index * group * NOPE, group * NOPE, 1)  19.8 us
    all_to_all x1, starting transfers between devices, per_device(): lax.all_to_all(outgoing, 'ctx', split_axis=0, concat_axis=0, tiled=True)  18.4 us
    dynamic_slice x8, local copies, waits for them, and re-layouts, group_out(): lax.dynamic_slice_in_dim(query_nope, index * group * NOPE, group * NOPE, 1)  14 us
  transfers between devices with their start and end apart: 5, of which 3 were waited for; matrix products, arithmetic and copies ran while one was open for 14% of the time, Pallas kernels for 0%

commit v1 on v0

v1 whole, which is shorter than its diff:
```python
import functools

import jax
import jax.numpy as jnp
from jax import lax
from jax.experimental import pallas as pl
from jax.experimental.pallas import tpu as pltpu
from jax.sharding import PartitionSpec as P

LATENT = 512
ROPE = 64
NOPE = 128
ROWS = 256
N_CTX = 32
N_HEAD = 8
SHARD = 32
BLOCKS = 5
SPAN = BLOCKS * ROWS
WINDOW = 1024
GROUPS = 8
SLOT = 8
DOCS = 8
FAR = -1e30
TO_EXP2 = 1.4426950408889634 / float(NOPE + ROPE) ** 0.5
MESH = pl.DeviceIdType.MESH
F32 = jnp.float32
BF16 = jnp.bfloat16


def iota(shape, dim):
    return lax.broadcasted_iota(jnp.int32, shape, dim)


def kernel(
    qn_hbm, qr_hbm, lat_hbm, ku_hbm, vu_hbm, docs, owner_ref, out_ref,
    qn, qr, ku, vu, stage, buf, kr, qbits, perm, place, outb, inb, idx_out, idx_in,
    load_sem, own_sem, gsend, grecv, fsend, isend, irecv, asend, arecv,
):
    c = lax.axis_index("ctx")
    h = lax.axis_index("head")
    k = lax.rem(c, 2)
    sibling = (c + 1 - 2 * k, h)

    def at(ahead, heads_on):
        return (lax.rem(c + ahead + N_CTX, N_CTX), lax.rem(h + heads_on, N_HEAD))

    lat_in = pltpu.make_async_copy(lat_hbm, stage, load_sem.at[0])
    lat_in.start()
    loads = [
        pltpu.make_async_copy(src, dst, load_sem.at[1 + i])
        for i, (src, dst) in enumerate(((ku_hbm, ku), (vu_hbm, vu), (qn_hbm, qn), (qr_hbm, qr)))
    ]
    for load in loads:
        load.start()

    barrier = pltpu.get_barrier_semaphore()

    def greet_ctx(i, carry):
        pl.semaphore_signal(barrier, inc=1, device_id=at(i, 0), device_id_type=MESH)
        return carry

    lax.fori_loop(1, N_CTX, greet_ctx, 0)

    def greet_head(j, carry):
        for ahead in (0, 2, -2, 4, -4):
            pl.semaphore_signal(barrier, inc=1, device_id=at(ahead, j), device_id_type=MESH)
        return carry

    lax.fori_loop(1, N_HEAD, greet_head, 0)
    pl.semaphore_wait(barrier, N_CTX - 1 + 5 * (N_HEAD - 1))

    lat_in.wait()
    own = pltpu.make_async_copy(stage, buf.at[4, h], grecv.at[4])
    own.start()
    for n, (ahead, slot, first) in enumerate(((2, 2, 0), (0, 4, 1), (4, 0, 0))):

        def spread(j, carry, n=n, ahead=ahead, slot=slot):
            pltpu.make_async_remote_copy(
                stage, buf.at[slot, h], gsend.at[n], grecv.at[slot],
                device_id=at(ahead, j), device_id_type=MESH,
            ).start()
            return carry

        lax.fori_loop(first, N_HEAD, spread, 0)

    owner = owner_ref[...]
    row = lax.shift_right_logical(owner, 8)
    place_row = jnp.bitwise_and(owner, ROWS - 1)
    step_row = jnp.bitwise_and(row - c + (2 * N_CTX - 1), N_CTX - 1)
    step_all = jnp.broadcast_to(step_row, (ROWS, ROWS))
    sub = iota((ROWS, ROWS), 0)
    lane = iota((ROWS, ROWS), 1)
    step_col = jnp.sum(jnp.where(sub == lane, step_all, 0), axis=1, keepdims=True)
    same = (step_col == step_row) & (sub < lane)
    rank = jnp.sum(jnp.where(same, 1, 0), axis=0, keepdims=True)
    slot_row = step_row * SLOT + rank
    hit = sub == slot_row
    perm[...] = jnp.where(hit, 1.0, 0.0).astype(BF16)
    place_col = jnp.sum(jnp.where(hit, place_row, 0), axis=1, keepdims=True)
    idx = jnp.broadcast_to(place_col, (ROWS, 128)).reshape(N_CTX, SLOT, 128)
    idx_out[...] = idx
    idx_in[N_CTX - 1] = idx[N_CTX - 1]

    def send_idx(i, carry):
        pltpu.make_async_remote_copy(
            idx_out.at[i], idx_in.at[i], isend, irecv,
            device_id=at(i + 1, 0), device_id_type=MESH,
        ).start()
        return carry

    lax.fori_loop(0, N_CTX - 1, send_idx, 0)

    lanes = iota((1, ROPE), 1)
    starts = jnp.zeros((1, ROPE), jnp.int32)
    ends = jnp.zeros((1, ROPE), jnp.int32)
    total = 0
    for d in range(DOCS):
        starts = jnp.where(lanes == d, total, starts)
        total = total + docs[d]
        ends = jnp.where(lanes == d, total, ends)
    key_pos = (c - 4) * ROWS + iota((SPAN, ROPE), 0)
    key_in = (key_pos >= starts) & (key_pos < ends)
    key_bits = jnp.where(key_in | (iota((SPAN, ROPE), 1) >= DOCS), 0.0, 1.0).astype(BF16)
    query_pos = c * ROWS + iota((ROWS, ROPE), 0)
    query_in = (query_pos >= starts) & (query_pos < ends)
    query_bits = jnp.where(query_in, FAR, 0.0)
    zeros = jnp.zeros((ROWS, ROPE), F32)
    ones = jnp.ones((ROWS, ROPE), F32)
    qbits[0] = jnp.concatenate([zeros, query_bits], axis=1).astype(BF16)
    qbits[1] = jnp.concatenate([query_bits, zeros], axis=1).astype(BF16)
    qbits[2] = jnp.concatenate([ones, zeros], axis=1).astype(BF16)
    qbits[3] = jnp.concatenate([zeros, ones], axis=1).astype(BF16)

    def arrived(slot):
        pltpu.make_async_copy(buf.at[slot], buf.at[slot], grecv.at[slot]).wait()

    def forward(src, dst, n):
        return pltpu.make_async_remote_copy(
            buf.at[src], buf.at[dst], fsend.at[n], grecv.at[dst],
            device_id=sibling, device_id_type=MESH,
        )

    arrived(2)
    first = forward(2, 2 * k + 1, 0)
    first.start()
    other = 4 - 4 * k
    arrived(other)
    second = forward(other, 3 - 2 * k, 1)
    second.start()
    arrived(4 * k)
    arrived(1)
    arrived(3)
    for load in loads:
        load.wait()

    rope = buf[:, :, :, LATENT:].reshape(SPAN, ROPE)
    kr[0] = jnp.concatenate([rope, key_bits], axis=1)
    kr[1] = jnp.concatenate([key_bits, rope], axis=1)

    lower = lane <= sub

    def attend(g, carry):
        cols = pl.ds(pl.multiple_of(g * 2 * NOPE, 2 * NOPE), 2 * NOPE)
        latent = buf[:, :, :, :LATENT].reshape(SPAN, LATENT)
        keys = jnp.dot(latent, ku[:, cols], preferred_element_type=F32).astype(BF16)
        values = jnp.dot(latent, vu[:, cols], preferred_element_type=F32).astype(BF16)
        q_two = qn[:, cols]
        r_two = qr[:, pl.ds(pl.multiple_of(g * 2 * ROPE, 2 * ROPE), 2 * ROPE)]
        outs = []
        for e in range(2):
            part = slice(e * NOPE, (e + 1) * NOPE)
            kx = jnp.concatenate([keys[:, part], kr[e]], axis=1)
            qx = jnp.concatenate([q_two[:, part], r_two * qbits[2 + e] + qbits[e]], axis=1)
            s = lax.dot_general(qx, kx, (((1,), (1,)), ((), ())), preferred_element_type=F32)
            s = jnp.concatenate(
                [
                    jnp.where(lower, FAR, s[:, :ROWS]),
                    s[:, ROWS:WINDOW],
                    jnp.where(lower, s[:, WINDOW:], FAR),
                ],
                axis=1,
            )
            largest = jnp.max(s, axis=1, keepdims=True)
            p = jnp.exp2((s - largest) * TO_EXP2)
            weight = jnp.sum(p, axis=1, keepdims=True)
            o = jnp.dot(p.astype(BF16), values[:, part], preferred_element_type=F32)
            outs.append((o / weight).astype(BF16))
        both = jnp.concatenate(outs, axis=1)
        sorted_ = jnp.dot(perm[...], both, preferred_element_type=F32)
        sorted_ = sorted_.reshape(N_CTX, SLOT, 2 * NOPE)
        packed = jnp.concatenate([sorted_[:, :, :NOPE], sorted_[:, :, NOPE:]], axis=1).astype(BF16)
        outb[g] = packed
        inb[g, N_CTX - 1] = packed[N_CTX - 1]

        def send(i, carry):
            pltpu.make_async_remote_copy(
                outb.at[g, i], inb.at[g, i], asend.at[g], arecv.at[g],
                device_id=at(i + 1, 0), device_id_type=MESH,
            ).start()
            return carry

        lax.fori_loop(0, N_CTX - 1, send, 0)
        return carry

    lax.fori_loop(0, GROUPS, attend, 0)

    rest = pl.ds(0, N_CTX - 1)
    pltpu.make_async_copy(idx_in.at[rest], idx_in.at[rest], irecv).wait()
    goal = idx_in[...].reshape(ROWS, 128)
    goal = jnp.concatenate([goal, goal], axis=1)
    place[...] = jnp.where(goal == lane, 1.0, 0.0).T.astype(BF16)

    def settle(g, carry):
        cols = pl.ds(pl.multiple_of(g * 2 * NOPE, 2 * NOPE), 2 * NOPE)
        pltpu.make_async_copy(inb.at[g, rest], inb.at[g, rest], arecv.at[g]).wait()
        got = inb[g].astype(F32)
        got = jnp.concatenate([got[:, :SLOT], got[:, SLOT:]], axis=2).reshape(ROWS, 2 * NOPE)
        out_ref[:, cols] = jnp.dot(
            place[...], got.astype(BF16), preferred_element_type=F32
        ).astype(BF16)
        return carry

    lax.fori_loop(0, GROUPS, settle, 0)

    def sent(ref, sem):
        pltpu.make_async_copy(ref, ref, sem).wait()

    sent(buf.at[0], gsend.at[0])
    sent(buf.at[0, pl.ds(0, N_HEAD - 1)], gsend.at[1])
    sent(buf.at[0], gsend.at[2])
    sent(buf.at[0], fsend.at[0])
    sent(buf.at[0], fsend.at[1])
    sent(idx_out.at[rest], isend)

    def all_sent(g, carry):
        sent(outb.at[g, rest], asend.at[g])
        return carry

    lax.fori_loop(0, GROUPS, all_sent, 0)


def per_device(query_nope, query_rope, latent, key_up, value_up, doc_lengths, owner):
    hbm = pl.BlockSpec(memory_space=pltpu.HBM)
    vmem = pl.BlockSpec(memory_space=pltpu.VMEM)
    dma = pltpu.SemaphoreType.DMA
    return pl.pallas_call(
        kernel,
        out_shape=jax.ShapeDtypeStruct(query_nope.shape, BF16),
        in_specs=[hbm] * 5 + [pl.BlockSpec(memory_space=pltpu.SMEM), vmem],
        out_specs=vmem,
        scratch_shapes=[
            pltpu.VMEM(query_nope.shape, BF16),
            pltpu.VMEM(query_rope.shape, BF16),
            pltpu.VMEM(key_up.shape, BF16),
            pltpu.VMEM(value_up.shape, BF16),
            pltpu.VMEM((SHARD, LATENT + ROPE), BF16),
            pltpu.VMEM((BLOCKS, N_HEAD, SHARD, LATENT + ROPE), BF16),
            pltpu.VMEM((2, SPAN, 2 * ROPE), BF16),
            pltpu.VMEM((4, ROWS, 2 * ROPE), BF16),
            pltpu.VMEM((ROWS, ROWS), BF16),
            pltpu.VMEM((ROWS, ROWS), BF16),
            pltpu.VMEM((GROUPS, N_CTX, 2 * SLOT, NOPE), BF16),
            pltpu.VMEM((GROUPS, N_CTX, 2 * SLOT, NOPE), BF16),
            pltpu.VMEM((N_CTX, SLOT, 128), jnp.int32),
            pltpu.VMEM((N_CTX, SLOT, 128), jnp.int32),
            dma((5,)),
            dma,
            dma((3,)),
            dma((5,)),
            dma((2,)),
            dma,
            dma,
            dma((GROUPS,)),
            dma((GROUPS,)),
        ],
        compiler_params=pltpu.CompilerParams(
            collective_id=0, has_side_effects=True, vmem_limit_bytes=62 << 20
        ),
        name="attend_and_place",
    )(query_nope, query_rope, latent, key_up, value_up, doc_lengths, owner.reshape(1, ROWS))


def solution(mesh):
    in_specs = (
        P("ctx", "head"),
        P("ctx", "head"),
        P(("ctx", "head"), None),
        P(None, "head"),
        P(None, "head"),
        P(),
        P("ctx"),
    )
    return jax.shard_map(
        per_device, mesh=mesh, in_specs=in_specs, out_specs=P("ctx", "head"), check_vma=False
    )
```

time: 299 us -> 63.1 us (0.21)
  local copies, waits for them, and re-layouts: 98.7 us -> 2.3 us
  blocking collectives: 80.8 us -> 0 us
  Pallas kernels: 0 us -> 60.6 us
  matrix products: 45.4 us -> 0 us
  starting transfers between devices: 39.1 us -> 0 us
  other arithmetic: 22.3 us -> 0 us
  waiting for transfers between devices: 10.6 us -> 0 us
    all_gather x2 -> x0, blocking collectives: 80.8 us -> none  [the longest x1 50.9 us: per_device(): owners_all = lax.all_gather(owner, 'ctx', axis=0, tiled=True)]
    pallas_call x0 -> x1, Pallas kernels: none -> 60.6 us  [per_device(): pl.pallas_call(kernel, out_shape=jax.ShapeDtypeStruct(query_nope.shape, B...]
    dynamic_slice x28 -> x0, local copies, waits for them, and re-layouts: 49.9 us -> none  [the longest x8 19.8 us: group_out(): lax.dynamic_slice_in_dim(keys_part, index * group * NOPE, group * NOPE, 1)]
    dot_general x14 -> x0, matrix products: 45.4 us -> none  [the longest x4 23.3 us: group_out(): jnp.einsum('hij,jhd->ihd', probs.astype(jnp.bfloat16), v_part, preferred_...]
    scatter x2 -> x0, local copies, waits for them, and re-layouts: 33.6 us -> none  [the longest x1 30.5 us: per_device(): jnp.zeros((every,), jnp.int32).at[owners_all]]
    ppermute x4 -> x0, starting transfers between devices: 20.7 us -> none  [from_behind(): return lax.ppermute(x, axis, pairs)]
    all_to_all x1 -> x0, starting transfers between devices: 18.4 us -> none  [per_device(): lax.all_to_all(outgoing, 'ctx', split_axis=0, concat_axis=0, tiled=True)]
    ppermute x4 -> x0, waiting for transfers between devices: 10.6 us -> none  [from_behind(): return lax.ppermute(x, axis, pairs)]
  transfers between devices with their start and end apart: 5 -> 0, of which waited for: 3 -> 0; matrix products, arithmetic and copies ran while one was open for 14% -> 0% of each run, Pallas kernels for 0% -> 0%
where the time goes in v1:
time: 63.1 us; the launch traced here: 62.9 us
  Pallas kernels  60.6 us (96%)
  local copies, waits for them, and re-layouts  2.3 us (4%)
    pallas_call x1, Pallas kernels, per_device(): pl.pallas_call(kernel, out_shape=jax.ShapeDtypeStruct(query_nope.shape, B...  60.6 us
    unnamed x1, local copies, waits for them, and re-layouts  2.3 us

profile of v1, /device:TPU:1, one launch (start us, length us, event | category | flops | bytes accessed | tf_op | source)
XLA Modules:
  0.0 62.9 jit_solution(7087950960235137596)
XLA Ops:
  0.0 60.6 %attend_and_place.1 = bf16[256,2048]{1,0:T(8,128)(2,1)} custom-call(bf16[256,2048]{1,0:T(8,128)(2,1)} %qn_hbm.1, bf16[256,1024]{1,0:T(8,128)(2,1)} %qr_hbm.1, bf16[32,576]{1,0:T(8,128)(2,1)} %lat_hbm.1, bf16[512,2048]{1,0:T(8,128)(2,1)} %ku_hbm.1, bf16[512,2048]{1,0:T(8,128)(2,1)} %vu_hbm.1, s32[8]{0:T(128)} %docs.1, s32[1,256]{1,0:T(1,128)} %bitcast.1), custom_call_target="tpu_custom_call" | custom-call | tf_op jit(solution)/shard_map/attend_and_place/pallas_call | solution.py:246
  60.6 2.3 %copy.9 = bf16[256,2048]{1,0:T(8,128)(2,1)} copy(bf16[256,2048]{1,0:T(8,128)(2,1)} %attend_and_place.1) | data formatting | bytes 2097152

commit v2 on v1

v2 whole, which is shorter than its diff:
```python
import functools

import jax
import jax.numpy as jnp
from jax import lax
from jax.experimental import pallas as pl
from jax.experimental.pallas import tpu as pltpu
from jax.sharding import PartitionSpec as P

LATENT = 512
ROPE = 64
NOPE = 128
ROWS = 256
N_CTX = 32
N_HEAD = 8
HALF = 16
BLOCKS = 5
SPAN = BLOCKS * ROWS
HALF_SPAN = SPAN // 2
WINDOW = 1024
GROUPS = 8
SLOT = 8
DOCS = 8
FAR = -1e30
TO_EXP2 = 1.4426950408889634 / float(NOPE + ROPE) ** 0.5
FAR_FIRST = sorted(range(1, N_CTX), key=lambda ahead: abs(ahead - N_CTX // 2))
MESH = pl.DeviceIdType.MESH
F32 = jnp.float32
BF16 = jnp.bfloat16


def iota(shape, dim):
    return lax.broadcasted_iota(jnp.int32, shape, dim)


def kernel(
    qn_hbm, qr_hbm, lat_hbm, ku_hbm, vu_hbm, docs_hbm, owner_hbm, out_ref,
    docs, owner_ref, qn, qr, ku, vu, buf, kr, qbits, perm, place, outb, inb, idx_out, idx_in,
    load_sem, lat_sem, x_send, y_send, row_send, pair_send, x_recv, y_recv, row_recv, pair_recv,
    fsend, frecv, isend, irecv, asend, arecv, near_sem, far_sem,
):
    c = lax.axis_index("ctx")
    h = lax.axis_index("head")
    k = jnp.bitwise_and(c, 1)
    x = h // 2
    yh = jnp.bitwise_and(h, 1)
    sibling = (c + 1 - 2 * k, h)

    def at(ahead):
        return (jnp.bitwise_and(c + ahead + N_CTX, N_CTX - 1), h)

    def across(ahead, flip):
        return (jnp.bitwise_and(c + ahead + N_CTX, N_CTX - 1), 2 * x + yh + flip - 2 * yh * flip)

    def along(j):
        return (c, 2 * jnp.bitwise_and(x + j, 3) + yh)

    def remote(src, dst, send, recv, to):
        return pltpu.make_async_remote_copy(
            src, dst, send, recv, device_id=to, device_id_type=MESH
        )

    def wait(ref, sem):
        pltpu.make_async_copy(ref, ref, sem).wait()

    own_row = buf.at[0, 4, pl.ds(4 * yh, 4)]
    own_a = buf.at[0, 4, 4 * yh + x]
    own_b = buf.at[1, 4, h]
    lat_in = [
        pltpu.make_async_copy(lat_hbm.at[pl.ds(HALF * i, HALF)], dst, lat_sem.at[i])
        for i, dst in enumerate((own_a, own_b))
    ]
    loads = [
        pltpu.make_async_copy(src, dst, load_sem.at[i])
        for i, (src, dst) in enumerate(
            (
                (owner_hbm, owner_ref), (docs_hbm, docs), (ku_hbm, ku), (vu_hbm, vu),
                (qn_hbm, qn), (qr_hbm, qr),
            )
        )
    ]
    for load in lat_in + loads:
        load.start()

    barrier = pltpu.get_barrier_semaphore()
    met = 0
    for plane in (0, -4, 4):
        for j in range(4):
            if plane or j:
                to = jnp.bitwise_and(c + plane + N_CTX, N_CTX - 4) + jnp.bitwise_and(c + j, 3)
                pl.semaphore_signal(barrier, inc=1, device_id=(to, h), device_id_type=MESH)
                met += 1
    for j in (1, 2, 3):
        pl.semaphore_signal(barrier, inc=1, device_id=along(j), device_id_type=MESH)
        met += 1
    for ahead in (0, 2, -2, 4, -4):
        pl.semaphore_signal(barrier, inc=1, device_id=across(ahead, 1), device_id_type=MESH)
        met += 1
    pl.semaphore_wait(barrier, met)
    for ahead in (4, -4):
        pl.semaphore_signal(near_sem, inc=1, device_id=at(ahead), device_id_type=MESH)

    for load in lat_in:
        load.wait()
    targets = [
        (n, ahead, slot, flip)
        for n, (ahead, slot, flip) in enumerate(
            ((2, 2, 0), (2, 2, 1), (4, 0, 0), (4, 0, 1), (0, 4, 1))
        )
    ]
    for n, ahead, slot, flip in targets:
        remote(own_b, buf.at[1, slot, h], y_send.at[n], y_recv.at[slot], across(ahead, flip)).start()
    for j in (1, 3, 2):
        remote(own_a, own_a, x_send.at[j - 1], x_recv, along(j)).start()

    wait(buf.at[0, 4, pl.ds(0, 3)], x_recv)
    for n, ahead, slot, flip in targets:
        remote(
            own_row, buf.at[0, slot, pl.ds(4 * yh, 4)], row_send.at[n], row_recv.at[slot],
            across(ahead, flip),
        ).start()
    for n, (slot, came) in enumerate(((2, 2), (4, 1), (0, 2))):
        wait(buf.at[1, slot, pl.ds(0, came)], y_recv.at[slot])
        pair = buf.at[1, slot, pl.ds(2 * x, 2)]
        for j in (1, 3, 2):
            remote(pair, pair, pair_send.at[3 * n + j - 1], pair_recv.at[slot], along(j)).start()

    pl.semaphore_wait(near_sem, 2)
    for ahead in (8, -8):
        pl.semaphore_signal(far_sem, inc=1, device_id=at(ahead), device_id_type=MESH)
    for load in loads[:2]:
        load.wait()
    owner = owner_ref[...]
    row = lax.shift_right_logical(owner, 8)
    place_row = jnp.bitwise_and(owner, ROWS - 1)
    step_row = jnp.bitwise_and(row - c + (2 * N_CTX - 1), N_CTX - 1)
    step_all = jnp.broadcast_to(step_row, (ROWS, ROWS))
    sub = iota((ROWS, ROWS), 0)
    lane = iota((ROWS, ROWS), 1)
    step_col = jnp.sum(jnp.where(sub == lane, step_all, 0), axis=1, keepdims=True)
    same = (step_col == step_row) & (sub < lane)
    rank = jnp.sum(jnp.where(same, 1, 0), axis=0, keepdims=True)
    slot_row = step_row * SLOT + rank
    hit = sub == slot_row
    perm[...] = jnp.where(hit, 1.0, 0.0).astype(BF16)
    place_col = jnp.sum(jnp.where(hit, place_row, 0), axis=1, keepdims=True)
    idx = jnp.broadcast_to(place_col, (ROWS, 128)).reshape(N_CTX, SLOT, 128)
    idx_out[...] = idx
    idx_in[N_CTX - 1] = idx[N_CTX - 1]

    lanes = iota((1, ROPE), 1)
    starts = jnp.zeros((1, ROPE), jnp.int32)
    ends = jnp.zeros((1, ROPE), jnp.int32)
    total = 0
    for d in range(DOCS):
        starts = jnp.where(lanes == d, total, starts)
        total = total + docs[d]
        ends = jnp.where(lanes == d, total, ends)
    step16 = iota((HALF_SPAN, ROPE), 0)
    within = jnp.bitwise_and(step16, 15)
    tile = jnp.bitwise_and(lax.shift_right_logical(step16, 4), 7)
    offset_a = jnp.bitwise_and(tile, 3) * 64 + lax.shift_right_logical(tile, 2) * 32 + within
    offset_b = tile * 32 + HALF + within
    block_pos = (c - 4 + lax.shift_right_logical(step16, 7)) * ROWS
    key_bits = []
    for offset in (offset_a, offset_b):
        key_pos = block_pos + offset
        key_in = (key_pos >= starts) & (key_pos < ends)
        key_bits.append(
            jnp.where(key_in | (iota((HALF_SPAN, ROPE), 1) >= DOCS), 0.0, 1.0).astype(BF16)
        )
    query_pos = c * ROWS + iota((ROWS, ROPE), 0)
    query_in = (query_pos >= starts) & (query_pos < ends)
    query_bits = jnp.where(query_in, FAR, 0.0)
    zeros = jnp.zeros((ROWS, ROPE), F32)
    ones = jnp.ones((ROWS, ROPE), F32)
    qbits[0] = jnp.concatenate([zeros, query_bits], axis=1).astype(BF16)
    qbits[1] = jnp.concatenate([query_bits, zeros], axis=1).astype(BF16)
    qbits[2] = jnp.concatenate([ones, zeros], axis=1).astype(BF16)
    qbits[3] = jnp.concatenate([zeros, ones], axis=1).astype(BF16)

    def forward(half, src, dst, n):
        remote(buf.at[half, src], buf.at[half, dst], fsend.at[n], frecv.at[n], sibling).start()

    wait(buf.at[0, 2], row_recv.at[2])
    forward(0, 2, 2 * k + 1, 0)
    wait(buf.at[1, 2, pl.ds(0, 6)], pair_recv.at[2])
    forward(1, 2, 2 * k + 1, 1)
    wait(buf.at[0, 4, pl.ds(0, 4)], row_recv.at[4])
    wait(buf.at[0, 0], row_recv.at[0])
    forward(0, 4 - 4 * k, 3 - 2 * k, 2)
    wait(buf.at[1, 4, pl.ds(0, 6)], pair_recv.at[4])
    wait(buf.at[1, 0, pl.ds(0, 6)], pair_recv.at[0])
    forward(1, 4 - 4 * k, 3 - 2 * k, 3)
    for n in range(4):
        wait(buf.at[0, 0], frecv.at[n])
    for load in loads[2:]:
        load.wait()

    for half in range(2):
        keys_here = pl.ds(half * HALF_SPAN, HALF_SPAN)
        rope = buf[half, :, :, :, LATENT:].reshape(HALF_SPAN, ROPE)
        kr[0, keys_here] = jnp.concatenate([rope, key_bits[half]], axis=1)
        kr[1, keys_here] = jnp.concatenate([key_bits[half], rope], axis=1)

    query_row = iota((ROWS, 128), 0)
    key_lane = iota((ROWS, 128), 1)
    within = jnp.bitwise_and(key_lane, 15)
    tile = lax.shift_right_logical(key_lane, 4)
    lower = [
        jnp.bitwise_and(tile, 3) * 64 + lax.shift_right_logical(tile, 2) * 32 + within <= query_row,
        tile * 32 + HALF + within <= query_row,
    ]

    def attend(g, carry):
        cols = pl.ds(pl.multiple_of(g * 2 * NOPE, 2 * NOPE), 2 * NOPE)
        latent = buf[:, :, :, :, :LATENT].reshape(SPAN, LATENT)
        keys = jnp.dot(latent, ku[:, cols], preferred_element_type=F32).astype(BF16)
        values = jnp.dot(latent, vu[:, cols], preferred_element_type=F32).astype(BF16)
        q_two = qn[:, cols]
        r_two = qr[:, pl.ds(pl.multiple_of(g * 2 * ROPE, 2 * ROPE), 2 * ROPE)]
        outs = []
        for e in range(2):
            part = slice(e * NOPE, (e + 1) * NOPE)
            kx = jnp.concatenate([keys[:, part], kr[e]], axis=1)
            qx = jnp.concatenate([q_two[:, part], r_two * qbits[2 + e] + qbits[e]], axis=1)
            s = lax.dot_general(qx, kx, (((1,), (1,)), ((), ())), preferred_element_type=F32)
            parts = []
            for half in range(2):
                first = half * HALF_SPAN
                parts += [
                    jnp.where(lower[half], FAR, s[:, first : first + 128]),
                    s[:, first + 128 : first + 512],
                    jnp.where(lower[half], s[:, first + 512 : first + 640], FAR),
                ]
            s = jnp.concatenate(parts, axis=1)
            largest = jnp.max(s, axis=1, keepdims=True)
            p = jnp.exp2((s - largest) * TO_EXP2)
            weight = jnp.sum(p, axis=1, keepdims=True)
            o = jnp.dot(p.astype(BF16), values[:, part], preferred_element_type=F32)
            outs.append((o / weight).astype(BF16))
        both = jnp.concatenate(outs, axis=1)
        sorted_ = jnp.dot(perm[...], both, preferred_element_type=F32)
        sorted_ = sorted_.reshape(N_CTX, SLOT, 2 * NOPE)
        packed = jnp.concatenate([sorted_[:, :, :NOPE], sorted_[:, :, NOPE:]], axis=1).astype(BF16)
        outb[g] = packed
        inb[g, N_CTX - 1] = packed[N_CTX - 1]

        @pl.when(g == 0)
        def first_sends():
            pl.semaphore_wait(far_sem, 2)
            for ahead in FAR_FIRST:
                remote(
                    idx_out.at[ahead - 1], idx_in.at[ahead - 1], isend, irecv, at(ahead)
                ).start()

        for ahead in FAR_FIRST:
            remote(
                outb.at[g, ahead - 1], inb.at[g, ahead - 1], asend.at[g], arecv.at[g], at(ahead)
            ).start()
        return carry

    lax.fori_loop(0, GROUPS, attend, 0)

    rest = pl.ds(0, N_CTX - 1)
    wait(idx_in.at[rest], irecv)
    goal = idx_in[...].reshape(ROWS, 128)
    goal = jnp.concatenate([goal, goal], axis=1)
    place[...] = jnp.where(goal == lane, 1.0, 0.0).T.astype(BF16)

    def settle(g, carry):
        cols = pl.ds(pl.multiple_of(g * 2 * NOPE, 2 * NOPE), 2 * NOPE)
        wait(inb.at[g, rest], arecv.at[g])
        got = inb[g].astype(F32)
        got = jnp.concatenate([got[:, :SLOT], got[:, SLOT:]], axis=2).reshape(ROWS, 2 * NOPE)
        out_ref[:, cols] = jnp.dot(
            place[...], got.astype(BF16), preferred_element_type=F32
        ).astype(BF16)
        return carry

    lax.fori_loop(0, GROUPS, settle, 0)

    for n in range(3):
        wait(own_a, x_send.at[n])
    for n in range(5):
        wait(own_b, y_send.at[n])
        wait(own_row, row_send.at[n])
    for n in range(9):
        wait(buf.at[1, 0, pl.ds(0, 2)], pair_send.at[n])
    for n in range(4):
        wait(buf.at[0, 0], fsend.at[n])
    wait(idx_out.at[rest], isend)

    def all_sent(g, carry):
        wait(outb.at[g, rest], asend.at[g])
        return carry

    lax.fori_loop(0, GROUPS, all_sent, 0)


def per_device(query_nope, query_rope, latent, key_up, value_up, doc_lengths, owner):
    hbm = pl.BlockSpec(memory_space=pltpu.HBM)
    dma = pltpu.SemaphoreType.DMA
    regular = pltpu.SemaphoreType.REGULAR
    args = (query_nope, query_rope, latent, key_up, value_up, doc_lengths, owner.reshape(1, ROWS))
    return pl.pallas_call(
        kernel,
        out_shape=pltpu.VMEM(query_nope.shape, BF16),
        in_specs=[hbm] * len(args),
        out_specs=pl.BlockSpec(memory_space=pltpu.VMEM),
        scratch_shapes=[
            pltpu.SMEM((DOCS,), jnp.int32),
            pltpu.VMEM((1, ROWS), jnp.int32),
            pltpu.VMEM(query_nope.shape, BF16),
            pltpu.VMEM(query_rope.shape, BF16),
            pltpu.VMEM(key_up.shape, BF16),
            pltpu.VMEM(value_up.shape, BF16),
            pltpu.VMEM((2, BLOCKS, N_HEAD, HALF, LATENT + ROPE), BF16),
            pltpu.VMEM((2, SPAN, 2 * ROPE), BF16),
            pltpu.VMEM((4, ROWS, 2 * ROPE), BF16),
            pltpu.VMEM((ROWS, ROWS), BF16),
            pltpu.VMEM((ROWS, ROWS), BF16),
            pltpu.VMEM((GROUPS, N_CTX, 2 * SLOT, NOPE), BF16),
            pltpu.VMEM((GROUPS, N_CTX, 2 * SLOT, NOPE), BF16),
            pltpu.VMEM((N_CTX, SLOT, 128), jnp.int32),
            pltpu.VMEM((N_CTX, SLOT, 128), jnp.int32),
            dma((6,)),
            dma((2,)),
            dma((3,)),
            dma((5,)),
            dma((5,)),
            dma((9,)),
            dma,
            dma((5,)),
            dma((5,)),
            dma((5,)),
            dma((4,)),
            dma((4,)),
            dma,
            dma,
            dma((GROUPS,)),
            dma((GROUPS,)),
            regular,
            regular,
        ],
        compiler_params=pltpu.CompilerParams(
            collective_id=0, has_side_effects=True, vmem_limit_bytes=48 << 20
        ),
        name="attend_and_place",
    )(*[pltpu.with_memory_space_constraint(a, pltpu.HBM) for a in args])


def solution(mesh):
    in_specs = (
        P("ctx", "head"),
        P("ctx", "head"),
        P(("ctx", "head"), None),
        P(None, "head"),
        P(None, "head"),
        P(),
        P("ctx"),
    )
    return jax.shard_map(
        per_device, mesh=mesh, in_specs=in_specs, out_specs=P("ctx", "head"), check_vma=False
    )
```

time: 63.1 us -> 56.3 us (0.89)
  Pallas kernels: 60.6 us -> 55.2 us
  local copies, waits for them, and re-layouts: 2.3 us -> 0.97 us
    pallas_call x1, Pallas kernels: 60.6 us -> 55.2 us  [per_device(): pl.pallas_call(kernel, out_shape=pltpu.VMEM(query_nope.shape, BF16), in_s...]
    unnamed x1, local copies, waits for them, and re-layouts: 2.3 us -> 0.97 us
where the time goes in v2:
time: 56.3 us; the launch traced here: 56.2 us
  Pallas kernels  55.2 us (98%)
  local copies, waits for them, and re-layouts  0.97 us (2%)
    pallas_call x1, Pallas kernels, per_device(): pl.pallas_call(kernel, out_shape=pltpu.VMEM(query_nope.shape, BF16), in_s...  55.2 us

profile of v2, /device:TPU:1, one launch (start us, length us, event | category | flops | bytes accessed | tf_op | source)
XLA Modules:
  0.0 56.2 jit_solution(16144218853526593091)
XLA Ops:
  0.0 55.2 %attend_and_place.1 = bf16[256,2048]{1,0:T(8,128)(2,1)S(1)} custom-call(bf16[256,2048]{1,0:T(8,128)(2,1)} %qn_hbm.1, bf16[256,1024]{1,0:T(8,128)(2,1)} %qr_hbm.1, bf16[32,576]{1,0:T(8,128)(2,1)} %lat_hbm.1, bf16[512,2048]{1,0:T(8,128)(2,1)} %ku_hbm.1, bf16[512,2048]{1,0:T(8,128)(2,1)} %vu_hbm.1, s32[8]{0:T(128)} %docs_hbm.1, s32[1,256]{1,0:T(1,128)} %bitcast.1), custom_call_target="tpu_custom_call" | custom-call | tf_op jit(solution)/shard_map/attend_and_place/pallas_call | solution.py:306
  55.2 1.0 %copy.9 = bf16[256,2048]{1,0:T(8,128)(2,1)} copy(bf16[256,2048]{1,0:T(8,128)(2,1)S(1)} %attend_and_place.1) | data formatting | bytes 2097152

commit v3 on v2

--- a/solution.py
+++ b/solution.py
@@ -63,7 +63,6 @@
     def wait(ref, sem):
         pltpu.make_async_copy(ref, ref, sem).wait()
 
-    own_row = buf.at[0, 4, pl.ds(4 * yh, 4)]
     own_a = buf.at[0, 4, 4 * yh + x]
     own_b = buf.at[1, 4, h]
     lat_in = [
@@ -108,22 +107,39 @@
             ((2, 2, 0), (2, 2, 1), (4, 0, 0), (4, 0, 1), (0, 4, 1))
         )
     ]
+    for j in (1, 3, 2):
+        remote(own_a, own_a, x_send.at[j - 1], x_recv.at[j - 1], along(j)).start()
     for n, ahead, slot, flip in targets:
-        remote(own_b, buf.at[1, slot, h], y_send.at[n], y_recv.at[slot], across(ahead, flip)).start()
-    for j in (1, 3, 2):
-        remote(own_a, own_a, x_send.at[j - 1], x_recv, along(j)).start()
-
-    wait(buf.at[0, 4, pl.ds(0, 3)], x_recv)
-    for n, ahead, slot, flip in targets:
-        remote(
-            own_row, buf.at[0, slot, pl.ds(4 * yh, 4)], row_send.at[n], row_recv.at[slot],
-            across(ahead, flip),
-        ).start()
-    for n, (slot, came) in enumerate(((2, 2), (4, 1), (0, 2))):
-        wait(buf.at[1, slot, pl.ds(0, came)], y_recv.at[slot])
-        pair = buf.at[1, slot, pl.ds(2 * x, 2)]
+        remote(own_b, buf.at[1, slot, h], y_send.at[n], y_recv.at[n], across(ahead, flip)).start()
+
+    def send_row(j):
+        from_x = 4 * yh + jnp.bitwise_and(x - j, 3)
+        if j:
+            wait(own_a, x_recv.at[j - 1])
+        for n, ahead, slot, flip in targets:
+            remote(
+                buf.at[0, 4, from_x], buf.at[0, slot, from_x], row_send.at[5 * j + n],
+                row_recv.at[slot], across(ahead, flip),
+            ).start()
+
+    def send_pair(n, slot, flip):
+        from_y = 2 * x + yh + flip - 2 * yh * flip
+        if n < 5:
+            wait(own_b, y_recv.at[n])
+        piece = buf.at[1, slot, from_y]
         for j in (1, 3, 2):
-            remote(pair, pair, pair_send.at[3 * n + j - 1], pair_recv.at[slot], along(j)).start()
+            remote(piece, piece, pair_send.at[3 * n + j - 1], pair_recv.at[slot], along(j)).start()
+
+    send_row(0)
+    send_pair(5, 4, 0)
+    send_row(1)
+    send_row(3)
+    send_pair(0, 2, 0)
+    send_pair(1, 2, 1)
+    send_pair(2, 0, 0)
+    send_pair(4, 4, 1)
+    send_row(2)
+    send_pair(3, 0, 1)
 
     pl.semaphore_wait(near_sem, 2)
     for ahead in (8, -8):
@@ -144,9 +160,16 @@
     hit = sub == slot_row
     perm[...] = jnp.where(hit, 1.0, 0.0).astype(BF16)
     place_col = jnp.sum(jnp.where(hit, place_row, 0), axis=1, keepdims=True)
-    idx = jnp.broadcast_to(place_col, (ROWS, 128)).reshape(N_CTX, SLOT, 128)
-    idx_out[...] = idx
-    idx_in[N_CTX - 1] = idx[N_CTX - 1]
+    place_slot = jnp.sum(jnp.where(sub == lane, place_col, 0), axis=0, keepdims=True)
+    half_sub = iota((N_CTX // 2, 128), 0)
+    half_lane = lax.shift_right_logical(iota((N_CTX // 2, 128), 1), 3)
+    for part in range(2):
+        spread = jnp.where(
+            half_sub == half_lane, place_slot[:, part * 128 : (part + 1) * 128], 0
+        )
+        for j in range(N_CTX // 2):
+            idx_out[part * N_CTX // 2 + j] = spread[j : j + 1]
+    idx_in[N_CTX - 1] = idx_out[N_CTX - 1]
 
     lanes = iota((1, ROPE), 1)
     starts = jnp.zeros((1, ROPE), jnp.int32)
@@ -264,9 +287,13 @@
 
     rest = pl.ds(0, N_CTX - 1)
     wait(idx_in.at[rest], irecv)
-    goal = idx_in[...].reshape(ROWS, 128)
-    goal = jnp.concatenate([goal, goal], axis=1)
-    place[...] = jnp.where(goal == lane, 1.0, 0.0).T.astype(BF16)
+    goals = []
+    for part in range(2):
+        goal = idx_in[part * N_CTX // 2]
+        for j in range(1, N_CTX // 2):
+            goal = goal + idx_in[part * N_CTX // 2 + j]
+        goals.append(goal)
+    place[...] = jnp.where(jnp.concatenate(goals, axis=1) == sub, 1.0, 0.0).astype(BF16)
 
     def settle(g, carry):
         cols = pl.ds(pl.multiple_of(g * 2 * NOPE, 2 * NOPE), 2 * NOPE)
@@ -284,9 +311,10 @@
         wait(own_a, x_send.at[n])
     for n in range(5):
         wait(own_b, y_send.at[n])
-        wait(own_row, row_send.at[n])
-    for n in range(9):
-        wait(buf.at[1, 0, pl.ds(0, 2)], pair_send.at[n])
+    for n in range(20):
+        wait(own_a, row_send.at[n])
+    for n in range(18):
+        wait(own_b, pair_send.at[n])
     for n in range(4):
         wait(buf.at[0, 0], fsend.at[n])
     wait(idx_out.at[rest], isend)
@@ -322,15 +350,15 @@
             pltpu.VMEM((ROWS, ROWS), BF16),
             pltpu.VMEM((GROUPS, N_CTX, 2 * SLOT, NOPE), BF16),
             pltpu.VMEM((GROUPS, N_CTX, 2 * SLOT, NOPE), BF16),
-            pltpu.VMEM((N_CTX, SLOT, 128), jnp.int32),
-            pltpu.VMEM((N_CTX, SLOT, 128), jnp.int32),
+            pltpu.VMEM((N_CTX, 1, 128), jnp.int32),
+            pltpu.VMEM((N_CTX, 1, 128), jnp.int32),
             dma((6,)),
             dma((2,)),
             dma((3,)),
             dma((5,)),
-            dma((5,)),
-            dma((9,)),
-            dma,
+            dma((20,)),
+            dma((18,)),
+            dma((3,)),
             dma((5,)),
             dma((5,)),
             dma((5,)),

time: 56.3 us -> 52.2 us (0.927)
  Pallas kernels: 55.2 us -> 51.1 us
    pallas_call x1, Pallas kernels: 55.2 us -> 51.1 us  [per_device(): pl.pallas_call(kernel, out_shape=pltpu.VMEM(query_nope.shape, BF16), in_s...]
where the time goes in v3:
time: 52.2 us; the launch traced here: 52.1 us
  Pallas kernels  51.1 us (98%)
  local copies, waits for them, and re-layouts  0.97 us (2%)
    pallas_call x1, Pallas kernels, per_device(): pl.pallas_call(kernel, out_shape=pltpu.VMEM(query_nope.shape, BF16), in_s...  51.1 us

profile of v3, /device:TPU:1, one launch (start us, length us, event | category | flops | bytes accessed | tf_op | source)
XLA Modules:
  0.0 52.1 jit_solution(2981999001315343362)
XLA Ops:
  0.0 51.1 %attend_and_place.1 = bf16[256,2048]{1,0:T(8,128)(2,1)S(1)} custom-call(bf16[256,2048]{1,0:T(8,128)(2,1)} %qn_hbm.1, bf16[256,1024]{1,0:T(8,128)(2,1)} %qr_hbm.1, bf16[32,576]{1,0:T(8,128)(2,1)} %lat_hbm.1, bf16[512,2048]{1,0:T(8,128)(2,1)} %ku_hbm.1, bf16[512,2048]{1,0:T(8,128)(2,1)} %vu_hbm.1, s32[8]{0:T(128)} %docs_hbm.1, s32[1,256]{1,0:T(1,128)} %bitcast.1), custom_call_target="tpu_custom_call" | custom-call | tf_op jit(solution)/shard_map/attend_and_place/pallas_call | solution.py:334
  51.1 1.0 %copy.9 = bf16[256,2048]{1,0:T(8,128)(2,1)} copy(bf16[256,2048]{1,0:T(8,128)(2,1)S(1)} %attend_and_place.1) | data formatting | bytes 2097152

commit v4 on v3

--- a/solution.py
+++ b/solution.py
@@ -35,7 +35,7 @@
 
 def kernel(
     qn_hbm, qr_hbm, lat_hbm, ku_hbm, vu_hbm, docs_hbm, owner_hbm, out_ref,
-    docs, owner_ref, qn, qr, ku, vu, buf, kr, qbits, perm, place, outb, inb, idx_out, idx_in,
+    docs, owner_ref, qn, qr, ku, vu, stage, buf0, buf1, kv, kr, qbits, perm, place, outb, inb, idx_out, idx_in,
     load_sem, lat_sem, x_send, y_send, row_send, pair_send, x_recv, y_recv, row_recv, pair_recv,
     fsend, frecv, isend, irecv, asend, arecv, near_sem, far_sem,
 ):
@@ -63,12 +63,9 @@
     def wait(ref, sem):
         pltpu.make_async_copy(ref, ref, sem).wait()
 
-    own_a = buf.at[0, 4, 4 * yh + x]
-    own_b = buf.at[1, 4, h]
-    lat_in = [
-        pltpu.make_async_copy(lat_hbm.at[pl.ds(HALF * i, HALF)], dst, lat_sem.at[i])
-        for i, dst in enumerate((own_a, own_b))
-    ]
+    own_a = buf0.at[4, 4 * yh + x]
+    own_b = buf1.at[4, h]
+    lat_in = pltpu.make_async_copy(lat_hbm, stage, lat_sem)
     loads = [
         pltpu.make_async_copy(src, dst, load_sem.at[i])
         for i, (src, dst) in enumerate(
@@ -78,7 +75,7 @@
             )
         )
     ]
-    for load in lat_in + loads:
+    for load in [lat_in] + loads:
         load.start()
 
     barrier = pltpu.get_barrier_semaphore()
@@ -99,8 +96,12 @@
     for ahead in (4, -4):
         pl.semaphore_signal(near_sem, inc=1, device_id=at(ahead), device_id_type=MESH)
 
-    for load in lat_in:
-        load.wait()
+    lat_in.wait()
+    rows = stage[...]
+    buf0[4, 4 * yh + x] = rows[:HALF, :LATENT]
+    buf1[4, h] = jnp.concatenate(
+        [rows[HALF:, :LATENT], rows[:HALF, LATENT:], rows[HALF:, LATENT:]], axis=1
+    )
     targets = [
         (n, ahead, slot, flip)
         for n, (ahead, slot, flip) in enumerate(
@@ -110,7 +111,7 @@
     for j in (1, 3, 2):
         remote(own_a, own_a, x_send.at[j - 1], x_recv.at[j - 1], along(j)).start()
     for n, ahead, slot, flip in targets:
-        remote(own_b, buf.at[1, slot, h], y_send.at[n], y_recv.at[n], across(ahead, flip)).start()
+        remote(own_b, buf1.at[slot, h], y_send.at[n], y_recv.at[n], across(ahead, flip)).start()
 
     def send_row(j):
         from_x = 4 * yh + jnp.bitwise_and(x - j, 3)
@@ -118,7 +119,7 @@
             wait(own_a, x_recv.at[j - 1])
         for n, ahead, slot, flip in targets:
             remote(
-                buf.at[0, 4, from_x], buf.at[0, slot, from_x], row_send.at[5 * j + n],
+                buf0.at[4, from_x], buf0.at[slot, from_x], row_send.at[5 * j + n],
                 row_recv.at[slot], across(ahead, flip),
             ).start()
 
@@ -126,7 +127,7 @@
         from_y = 2 * x + yh + flip - 2 * yh * flip
         if n < 5:
             wait(own_b, y_recv.at[n])
-        piece = buf.at[1, slot, from_y]
+        piece = buf1.at[slot, from_y]
         for j in (1, 3, 2):
             remote(piece, piece, pair_send.at[3 * n + j - 1], pair_recv.at[slot], along(j)).start()
 
@@ -134,6 +135,9 @@
     send_pair(5, 4, 0)
     send_row(1)
     send_row(3)
+    pl.semaphore_wait(near_sem, 2)
+    for ahead in (8, -8):
+        pl.semaphore_signal(far_sem, inc=1, device_id=at(ahead), device_id_type=MESH)
     send_pair(0, 2, 0)
     send_pair(1, 2, 1)
     send_pair(2, 0, 0)
@@ -141,9 +145,6 @@
     send_row(2)
     send_pair(3, 0, 1)
 
-    pl.semaphore_wait(near_sem, 2)
-    for ahead in (8, -8):
-        pl.semaphore_signal(far_sem, inc=1, device_id=at(ahead), device_id_type=MESH)
     for load in loads[:2]:
         load.wait()
     owner = owner_ref[...]
@@ -202,29 +203,58 @@
     qbits[2] = jnp.concatenate([ones, zeros], axis=1).astype(BF16)
     qbits[3] = jnp.concatenate([zeros, ones], axis=1).astype(BF16)
 
-    def forward(half, src, dst, n):
-        remote(buf.at[half, src], buf.at[half, dst], fsend.at[n], frecv.at[n], sibling).start()
-
-    wait(buf.at[0, 2], row_recv.at[2])
-    forward(0, 2, 2 * k + 1, 0)
-    wait(buf.at[1, 2, pl.ds(0, 6)], pair_recv.at[2])
-    forward(1, 2, 2 * k + 1, 1)
-    wait(buf.at[0, 4, pl.ds(0, 4)], row_recv.at[4])
-    wait(buf.at[0, 0], row_recv.at[0])
-    forward(0, 4 - 4 * k, 3 - 2 * k, 2)
-    wait(buf.at[1, 4, pl.ds(0, 6)], pair_recv.at[4])
-    wait(buf.at[1, 0, pl.ds(0, 6)], pair_recv.at[0])
-    forward(1, 4 - 4 * k, 3 - 2 * k, 3)
-    for n in range(4):
-        wait(buf.at[0, 0], frecv.at[n])
+    def forward(buf, src, dst, n):
+        remote(buf.at[src], buf.at[dst], fsend.at[n], frecv.at[n], sibling).start()
+
+    def prepare(slot):
+        latent = latents((slot,))
+        cols = slice(0, 2 * NOPE)
+        keys = jnp.dot(latent, ku[:, cols], preferred_element_type=F32).astype(BF16)
+        values = jnp.dot(latent, vu[:, cols], preferred_element_type=F32).astype(BF16)
+        rope = buf1[slot, :, :, LATENT:]
+        for half in range(2):
+            here = pl.ds(half * HALF_SPAN + slot * 128, 128)
+            part = slice(half * 128, (half + 1) * 128)
+            kv[0, 0, here] = keys[part]
+            kv[0, 1, here] = values[part]
+            if half == 0:
+                rotary = jnp.concatenate([rope[n] for n in (0, 2, 4, 6, 1, 3, 5, 7)], axis=0)
+            else:
+                rotary = rope.reshape(128, 2 * ROPE)
+            rotary = rotary[:, half * ROPE : (half + 1) * ROPE]
+            bits = key_bits[half][slot * 128 : (slot + 1) * 128]
+            kr[0, here] = jnp.concatenate([rotary, bits], axis=1)
+            kr[1, here] = jnp.concatenate([bits, rotary], axis=1)
+
+    def latents(slots):
+        return jnp.concatenate(
+            [buf0[s].reshape(128, LATENT) for s in slots]
+            + [buf1[s, :, :, :LATENT].reshape(128, LATENT) for s in slots],
+            axis=0,
+        )
+
+    wait(buf0.at[2], row_recv.at[2])
+    forward(buf0, 2, 2 * k + 1, 0)
+    wait(buf1.at[2, pl.ds(0, 6)], pair_recv.at[2])
+    forward(buf1, 2, 2 * k + 1, 1)
+    wait(buf0.at[4, pl.ds(0, 4)], row_recv.at[4])
+    wait(buf0.at[0], row_recv.at[0])
+    forward(buf0, 4 - 4 * k, 3 - 2 * k, 2)
+    wait(buf1.at[4, pl.ds(0, 6)], pair_recv.at[4])
+    wait(buf1.at[0, pl.ds(0, 6)], pair_recv.at[0])
+    forward(buf1, 4 - 4 * k, 3 - 2 * k, 3)
+
+    pl.semaphore_wait(far_sem, 2)
+    for ahead in FAR_FIRST:
+        remote(idx_out.at[ahead - 1], idx_in.at[ahead - 1], isend, irecv, at(ahead)).start()
     for load in loads[2:]:
         load.wait()
-
-    for half in range(2):
-        keys_here = pl.ds(half * HALF_SPAN, HALF_SPAN)
-        rope = buf[half, :, :, :, LATENT:].reshape(HALF_SPAN, ROPE)
-        kr[0, keys_here] = jnp.concatenate([rope, key_bits[half]], axis=1)
-        kr[1, keys_here] = jnp.concatenate([key_bits[half], rope], axis=1)
+    for slot in (2, 4, 0):
+        prepare(slot)
+    for n in range(4):
+        wait((buf0, buf1)[n % 2].at[0], frecv.at[n])
+    for slot in (1, 3):
+        prepare(slot)
 
     query_row = iota((ROWS, 128), 0)
     key_lane = iota((ROWS, 128), 1)
@@ -237,9 +267,9 @@
 
     def attend(g, carry):
         cols = pl.ds(pl.multiple_of(g * 2 * NOPE, 2 * NOPE), 2 * NOPE)
-        latent = buf[:, :, :, :, :LATENT].reshape(SPAN, LATENT)
-        keys = jnp.dot(latent, ku[:, cols], preferred_element_type=F32).astype(BF16)
-        values = jnp.dot(latent, vu[:, cols], preferred_element_type=F32).astype(BF16)
+        now = jnp.bitwise_and(g, 1)
+        keys = kv[now, 0]
+        values = kv[now, 1]
         q_two = qn[:, cols]
         r_two = qr[:, pl.ds(pl.multiple_of(g * 2 * ROPE, 2 * ROPE), 2 * ROPE)]
         outs = []
@@ -269,18 +299,31 @@
         outb[g] = packed
         inb[g, N_CTX - 1] = packed[N_CTX - 1]
 
-        @pl.when(g == 0)
-        def first_sends():
-            pl.semaphore_wait(far_sem, 2)
-            for ahead in FAR_FIRST:
-                remote(
-                    idx_out.at[ahead - 1], idx_in.at[ahead - 1], isend, irecv, at(ahead)
-                ).start()
-
-        for ahead in FAR_FIRST:
+        def send(ahead):
             remote(
                 outb.at[g, ahead - 1], inb.at[g, ahead - 1], asend.at[g], arecv.at[g], at(ahead)
             ).start()
+
+        @pl.when(g < GROUPS - 1)
+        def far_first():
+            for ahead in FAR_FIRST:
+                send(ahead)
+
+        @pl.when(g == GROUPS - 1)
+        def in_order():
+            for to in range(N_CTX):
+
+                @pl.when(c != to)
+                def send_to(to=to):
+                    send(jnp.bitwise_and(to - c, N_CTX - 1))
+
+        following = jnp.minimum(g + 1, GROUPS - 1) * 2 * NOPE
+        cols = pl.ds(pl.multiple_of(following, 2 * NOPE), 2 * NOPE)
+        latent = latents(range(BLOCKS))
+        keys = jnp.dot(latent, ku[:, cols], preferred_element_type=F32)
+        kv[1 - now, 0] = keys.astype(BF16)
+        values = jnp.dot(latent, vu[:, cols], preferred_element_type=F32)
+        kv[1 - now, 1] = values.astype(BF16)
         return carry
 
     lax.fori_loop(0, GROUPS, attend, 0)
@@ -316,7 +359,7 @@
     for n in range(18):
         wait(own_b, pair_send.at[n])
     for n in range(4):
-        wait(buf.at[0, 0], fsend.at[n])
+        wait((buf0, buf1)[n % 2].at[0], fsend.at[n])
     wait(idx_out.at[rest], isend)
 
     def all_sent(g, carry):
@@ -343,7 +386,10 @@
             pltpu.VMEM(query_rope.shape, BF16),
             pltpu.VMEM(key_up.shape, BF16),
             pltpu.VMEM(value_up.shape, BF16),
-            pltpu.VMEM((2, BLOCKS, N_HEAD, HALF, LATENT + ROPE), BF16),
+            pltpu.VMEM((2 * HALF, LATENT + ROPE), BF16),
+            pltpu.VMEM((BLOCKS, N_HEAD, HALF, LATENT), BF16),
+            pltpu.VMEM((BLOCKS, N_HEAD, HALF, LATENT + 2 * ROPE), BF16),
+            pltpu.VMEM((2, 2, SPAN, 2 * NOPE), BF16),
             pltpu.VMEM((2, SPAN, 2 * ROPE), BF16),
             pltpu.VMEM((4, ROWS, 2 * ROPE), BF16),
             pltpu.VMEM((ROWS, ROWS), BF16),
@@ -353,7 +399,7 @@
             pltpu.VMEM((N_CTX, 1, 128), jnp.int32),
             pltpu.VMEM((N_CTX, 1, 128), jnp.int32),
             dma((6,)),
-            dma((2,)),
+            dma,
             dma((3,)),
             dma((5,)),
             dma((20,)),

time: 52.2 us -> 49.8 us (0.954)
  Pallas kernels: 51.1 us -> 48.7 us
    pallas_call x1, Pallas kernels: 51.1 us -> 48.7 us  [per_device(): pl.pallas_call(kernel, out_shape=pltpu.VMEM(query_nope.shape, BF16), in_s...]
where the time goes in v4:
time: 49.8 us; the launch traced here: 49.7 us
  Pallas kernels  48.7 us (98%)
  local copies, waits for them, and re-layouts  0.97 us (2%)
    pallas_call x1, Pallas kernels, per_device(): pl.pallas_call(kernel, out_shape=pltpu.VMEM(query_nope.shape, BF16), in_s...  48.7 us

profile of v4, /device:TPU:1, one launch (start us, length us, event | category | flops | bytes accessed | tf_op | source)
XLA Modules:
  0.0 49.7 jit_solution(6767970055328395725)
XLA Ops:
  0.0 48.7 %attend_and_place.1 = bf16[256,2048]{1,0:T(8,128)(2,1)S(1)} custom-call(bf16[256,2048]{1,0:T(8,128)(2,1)} %qn_hbm.1, bf16[256,1024]{1,0:T(8,128)(2,1)} %qr_hbm.1, bf16[32,576]{1,0:T(8,128)(2,1)} %lat_hbm.1, bf16[512,2048]{1,0:T(8,128)(2,1)} %ku_hbm.1, bf16[512,2048]{1,0:T(8,128)(2,1)} %vu_hbm.1, s32[8]{0:T(128)} %docs_hbm.1, s32[1,256]{1,0:T(1,128)} %bitcast.1), custom_call_target="tpu_custom_call" | custom-call | tf_op jit(solution)/shard_map/attend_and_place/pallas_call | solution.py:377
  48.7 1.0 %copy.9 = bf16[256,2048]{1,0:T(8,128)(2,1)} copy(bf16[256,2048]{1,0:T(8,128)(2,1)S(1)} %attend_and_place.1) | data formatting | bytes 2097152

commit v5 on v4

--- a/solution.py
+++ b/solution.py
@@ -35,7 +35,7 @@
 
 def kernel(
     qn_hbm, qr_hbm, lat_hbm, ku_hbm, vu_hbm, docs_hbm, owner_hbm, out_ref,
-    docs, owner_ref, qn, qr, ku, vu, stage, buf0, buf1, kv, kr, qbits, perm, place, outb, inb, idx_out, idx_in,
+    docs, owner_ref, qn, qr, ku, vu, stage, buf0, buf1, kv, kr, kbits, qbits, perm, place, outb, inb, idx_out, idx_in,
     load_sem, lat_sem, x_send, y_send, row_send, pair_send, x_recv, y_recv, row_recv, pair_recv,
     fsend, frecv, isend, irecv, asend, arecv, near_sem, far_sem,
 ):
@@ -186,13 +186,12 @@
     offset_a = jnp.bitwise_and(tile, 3) * 64 + lax.shift_right_logical(tile, 2) * 32 + within
     offset_b = tile * 32 + HALF + within
     block_pos = (c - 4 + lax.shift_right_logical(step16, 7)) * ROWS
-    key_bits = []
-    for offset in (offset_a, offset_b):
+    for half, offset in enumerate((offset_a, offset_b)):
         key_pos = block_pos + offset
         key_in = (key_pos >= starts) & (key_pos < ends)
-        key_bits.append(
-            jnp.where(key_in | (iota((HALF_SPAN, ROPE), 1) >= DOCS), 0.0, 1.0).astype(BF16)
-        )
+        kbits[half] = jnp.where(
+            key_in | (iota((HALF_SPAN, ROPE), 1) >= DOCS), 0.0, 1.0
+        ).astype(BF16)
     query_pos = c * ROWS + iota((ROWS, ROPE), 0)
     query_in = (query_pos >= starts) & (query_pos < ends)
     query_bits = jnp.where(query_in, FAR, 0.0)
@@ -213,7 +212,7 @@
         values = jnp.dot(latent, vu[:, cols], preferred_element_type=F32).astype(BF16)
         rope = buf1[slot, :, :, LATENT:]
         for half in range(2):
-            here = pl.ds(half * HALF_SPAN + slot * 128, 128)
+            here = pl.ds(pl.multiple_of(half * HALF_SPAN + slot * 128, 128), 128)
             part = slice(half * 128, (half + 1) * 128)
             kv[0, 0, here] = keys[part]
             kv[0, 1, here] = values[part]
@@ -222,7 +221,7 @@
             else:
                 rotary = rope.reshape(128, 2 * ROPE)
             rotary = rotary[:, half * ROPE : (half + 1) * ROPE]
-            bits = key_bits[half][slot * 128 : (slot + 1) * 128]
+            bits = kbits[half, pl.ds(pl.multiple_of(slot * 128, 128), 128)]
             kr[0, here] = jnp.concatenate([rotary, bits], axis=1)
             kr[1, here] = jnp.concatenate([bits, rotary], axis=1)
 
@@ -237,23 +236,24 @@
     forward(buf0, 2, 2 * k + 1, 0)
     wait(buf1.at[2, pl.ds(0, 6)], pair_recv.at[2])
     forward(buf1, 2, 2 * k + 1, 1)
+    for load in loads[2:]:
+        load.wait()
+    prepare(2)
     wait(buf0.at[4, pl.ds(0, 4)], row_recv.at[4])
     wait(buf0.at[0], row_recv.at[0])
     forward(buf0, 4 - 4 * k, 3 - 2 * k, 2)
     wait(buf1.at[4, pl.ds(0, 6)], pair_recv.at[4])
+    prepare(4)
     wait(buf1.at[0, pl.ds(0, 6)], pair_recv.at[0])
     forward(buf1, 4 - 4 * k, 3 - 2 * k, 3)
 
     pl.semaphore_wait(far_sem, 2)
     for ahead in FAR_FIRST:
         remote(idx_out.at[ahead - 1], idx_in.at[ahead - 1], isend, irecv, at(ahead)).start()
-    for load in loads[2:]:
-        load.wait()
-    for slot in (2, 4, 0):
-        prepare(slot)
-    for n in range(4):
-        wait((buf0, buf1)[n % 2].at[0], frecv.at[n])
-    for slot in (1, 3):
+    prepare(0)
+    for n, slot in ((0, 3 - 2 * k), (2, 2 * k + 1)):
+        wait(buf0.at[0], frecv.at[n])
+        wait(buf1.at[0], frecv.at[n + 1])
         prepare(slot)
 
     query_row = iota((ROWS, 128), 0)
@@ -391,6 +391,7 @@
             pltpu.VMEM((BLOCKS, N_HEAD, HALF, LATENT + 2 * ROPE), BF16),
             pltpu.VMEM((2, 2, SPAN, 2 * NOPE), BF16),
             pltpu.VMEM((2, SPAN, 2 * ROPE), BF16),
+            pltpu.VMEM((2, HALF_SPAN, ROPE), BF16),
             pltpu.VMEM((4, ROWS, 2 * ROPE), BF16),
             pltpu.VMEM((ROWS, ROWS), BF16),
             pltpu.VMEM((ROWS, ROWS), BF16),

time: 49.8 us -> 49.7 us (level)
  no operation moved by 1% of the time
where the time goes in v5:
time: 49.7 us; the launch traced here: 49.6 us
  Pallas kernels  48.6 us (98%)
  local copies, waits for them, and re-layouts  0.97 us (2%)
    pallas_call x1, Pallas kernels, per_device(): pl.pallas_call(kernel, out_shape=pltpu.VMEM(query_nope.shape, BF16), in_s...  48.6 us

profile of v5, /device:TPU:1, one launch (start us, length us, event | category | flops | bytes accessed | tf_op | source)
XLA Modules:
  0.0 49.6 jit_solution(14146971908763402534)
XLA Ops:
  0.0 48.6 %attend_and_place.1 = bf16[256,2048]{1,0:T(8,128)(2,1)S(1)} custom-call(bf16[256,2048]{1,0:T(8,128)(2,1)} %qn_hbm.1, bf16[256,1024]{1,0:T(8,128)(2,1)} %qr_hbm.1, bf16[32,576]{1,0:T(8,128)(2,1)} %lat_hbm.1, bf16[512,2048]{1,0:T(8,128)(2,1)} %ku_hbm.1, bf16[512,2048]{1,0:T(8,128)(2,1)} %vu_hbm.1, s32[8]{0:T(128)} %docs_hbm.1, s32[1,256]{1,0:T(1,128)} %bitcast.1), custom_call_target="tpu_custom_call" | custom-call | tf_op jit(solution)/shard_map/attend_and_place/pallas_call | solution.py:377
  48.6 1.0 %copy.9 = bf16[256,2048]{1,0:T(8,128)(2,1)} copy(bf16[256,2048]{1,0:T(8,128)(2,1)S(1)} %attend_and_place.1) | data formatting | bytes 2097152

commit v6 on v5

--- a/solution.py
+++ b/solution.py
@@ -24,6 +24,7 @@
 FAR = -1e30
 TO_EXP2 = 1.4426950408889634 / float(NOPE + ROPE) ** 0.5
 FAR_FIRST = sorted(range(1, N_CTX), key=lambda ahead: abs(ahead - N_CTX // 2))
+RELAYED = {5: 1, 0: 3}
 MESH = pl.DeviceIdType.MESH
 F32 = jnp.float32
 BF16 = jnp.bfloat16
@@ -36,7 +37,7 @@
 def kernel(
     qn_hbm, qr_hbm, lat_hbm, ku_hbm, vu_hbm, docs_hbm, owner_hbm, out_ref,
     docs, owner_ref, qn, qr, ku, vu, stage, buf0, buf1, kv, kr, kbits, qbits, perm, place, outb, inb, idx_out, idx_in,
-    load_sem, lat_sem, x_send, y_send, row_send, pair_send, x_recv, y_recv, row_recv, pair_recv,
+    load_sem, lat_sem, x_send, y_send, row_send, pair_send, x_recv, y_recv, row_recv, pair_recv, relay_recv,
     fsend, frecv, isend, irecv, asend, arecv, near_sem, far_sem,
 ):
     c = lax.axis_index("ctx")
@@ -128,8 +129,18 @@
         if n < 5:
             wait(own_b, y_recv.at[n])
         piece = buf1.at[slot, from_y]
+        way = RELAYED.get(n, 0)
         for j in (1, 3, 2):
-            remote(piece, piece, pair_send.at[3 * n + j - 1], pair_recv.at[slot], along(j)).start()
+            if way and j == 2:
+                continue
+            landed = relay_recv.at[way // 2] if j == way else pair_recv.at[slot]
+            remote(piece, piece, pair_send.at[3 * n + j - 1], landed, along(j)).start()
+
+    def relay(n, slot):
+        way = RELAYED[n]
+        wait(own_b, relay_recv.at[way // 2])
+        piece = buf1.at[slot, 2 * jnp.bitwise_and(x - way, 3) + yh]
+        remote(piece, piece, pair_send.at[3 * n + 1], pair_recv.at[slot], along(way)).start()
 
     send_row(0)
     send_pair(5, 4, 0)
@@ -139,9 +150,11 @@
     for ahead in (8, -8):
         pl.semaphore_signal(far_sem, inc=1, device_id=at(ahead), device_id_type=MESH)
     send_pair(0, 2, 0)
+    relay(5, 4)
     send_pair(1, 2, 1)
     send_pair(2, 0, 0)
     send_pair(4, 4, 1)
+    relay(0, 2)
     send_row(2)
     send_pair(3, 0, 1)
 
@@ -234,7 +247,7 @@
 
     wait(buf0.at[2], row_recv.at[2])
     forward(buf0, 2, 2 * k + 1, 0)
-    wait(buf1.at[2, pl.ds(0, 6)], pair_recv.at[2])
+    wait(buf1.at[2, pl.ds(0, 5)], pair_recv.at[2])
     forward(buf1, 2, 2 * k + 1, 1)
     for load in loads[2:]:
         load.wait()
@@ -242,7 +255,7 @@
     wait(buf0.at[4, pl.ds(0, 4)], row_recv.at[4])
     wait(buf0.at[0], row_recv.at[0])
     forward(buf0, 4 - 4 * k, 3 - 2 * k, 2)
-    wait(buf1.at[4, pl.ds(0, 6)], pair_recv.at[4])
+    wait(buf1.at[4, pl.ds(0, 5)], pair_recv.at[4])
     prepare(4)
     wait(buf1.at[0, pl.ds(0, 6)], pair_recv.at[0])
     forward(buf1, 4 - 4 * k, 3 - 2 * k, 3)
@@ -409,6 +422,7 @@
             dma((5,)),
             dma((5,)),
             dma((5,)),
+            dma((2,)),
             dma((4,)),
             dma((4,)),
             dma,

time: 49.7 us -> 50.9 us (1.024)
  Pallas kernels: 48.6 us -> 49.9 us
    pallas_call x1, Pallas kernels: 48.6 us -> 49.9 us  [per_device(): pl.pallas_call(kernel, out_shape=pltpu.VMEM(query_nope.shape, BF16), in_s...]
where the time goes in v6:
time: 50.9 us
  Pallas kernels  49.9 us (98%)
  local copies, waits for them, and re-layouts  0.97 us (2%)
    pallas_call x1, Pallas kernels, per_device(): pl.pallas_call(kernel, out_shape=pltpu.VMEM(query_nope.shape, BF16), in_s...  49.9 us

profile of v6, /device:TPU:1, one launch (start us, length us, event | category | flops | bytes accessed | tf_op | source)
XLA Modules:
  0.0 50.9 jit_solution(6397079695435215385)
XLA Ops:
  0.0 49.9 %attend_and_place.1 = bf16[256,2048]{1,0:T(8,128)(2,1)S(1)} custom-call(bf16[256,2048]{1,0:T(8,128)(2,1)} %qn_hbm.1, bf16[256,1024]{1,0:T(8,128)(2,1)} %qr_hbm.1, bf16[32,576]{1,0:T(8,128)(2,1)} %lat_hbm.1, bf16[512,2048]{1,0:T(8,128)(2,1)} %ku_hbm.1, bf16[512,2048]{1,0:T(8,128)(2,1)} %vu_hbm.1, s32[8]{0:T(128)} %docs_hbm.1, s32[1,256]{1,0:T(1,128)} %bitcast.1), custom_call_target="tpu_custom_call" | custom-call | tf_op jit(solution)/shard_map/attend_and_place/pallas_call | solution.py:390
  49.9 1.0 %copy.9 = bf16[256,2048]{1,0:T(8,128)(2,1)} copy(bf16[256,2048]{1,0:T(8,128)(2,1)S(1)} %attend_and_place.1) | data formatting | bytes 2097152
